TPU v7x, 32 devices: a whole 2x2x4 slice. The times are simulated.
32 devices in a mesh: layer: 8 (over z, y), blk: 4 (over x, core).
Axes of the slice: x: 2, y: 2, z: 4, core: 2. Of those that a mesh axis runs over, the one named last changes fastest.
Arguments:
- mode_matrix: bfloat16 [16, 512, 512], P(None, 'layer', 'blk'), may hold values from -1 to 1, as said below
- decay_rate: bfloat16 [16, 512], P(None, 'layer'), may hold values from 0.0009994507 to 0.29882812
- facet_refl: bfloat16 [16, 512], P(None, 'layer'), may hold values from -0.796875 to 0.796875
Outputs:
- prefix: bfloat16 [8, 4, 512, 512], P('layer', None, 'blk')
Inputs may be any that keep to these rules, and one draw needn't show every extreme that they name: `mode_matrix`: each layer's matrix has orthonormal columns up to the rounding to bfloat16.
All inputs are finite; a program needn't handle non-finite values.
Results may differ from a plain program's by a relative error of at most 0.0045.
The roundings to bfloat16 on the way count: a program that leaves them out, or rounds other values in their place, can miss the bound.
Values may be sent and summed in bfloat16 or wider, within the bound.
A program may use at most 64 MiB of HBM per device.

v0:
```python
import jax
import jax.numpy as jnp
from jax import lax
from jax.sharding import PartitionSpec as P

HARM = 512
REFL = 4


def passed_along(value, axis, steps):
    count = lax.axis_size(axis)
    first, last = (max(0, -steps), min(count, count - steps))
    return lax.ppermute(value, axis, [(source, source + steps) for source in range(first, last)])


def times_f32(left_op, right_op):
    return jnp.dot(left_op, right_op, preferred_element_type=jnp.float32)


def star_rows(upper_near, upper_far, lower_near, lower_rows):
    coupling_down = times_f32(lower_near[0], upper_far[1]).astype(jnp.bfloat16)
    coupling_up = times_f32(upper_far[1], lower_near[0]).astype(jnp.bfloat16)
    left_sum = upper_near[1]
    for repeat in range(REFL):
        left_sum = (upper_near[1] + times_f32(left_sum, coupling_down)).astype(jnp.bfloat16)
    right_sum = lower_rows[0]
    for repeat in range(REFL):
        right_sum = (lower_rows[0] + times_f32(right_sum, coupling_up)).astype(jnp.bfloat16)
    left_mid = times_f32(left_sum, lower_near[0]).astype(jnp.bfloat16)
    right_mid = times_f32(right_sum, upper_far[1]).astype(jnp.bfloat16)
    new_refl = (upper_near[0] + times_f32(left_mid, upper_far[0])).astype(jnp.bfloat16)
    new_back = times_f32(left_sum, lower_near[1]).astype(jnp.bfloat16)
    new_fore = times_f32(right_sum, upper_far[0]).astype(jnp.bfloat16)
    new_under = (lower_rows[1] + times_f32(right_mid, lower_near[1])).astype(jnp.bfloat16)
    return jnp.stack([new_refl, new_back, new_fore, new_under])


def on_device(mode_matrix, decay_rate, facet_refl):
    relayed_modes, relayed_decay, relayed_refl = (
        lax.all_to_all(mode_matrix, "layer", split_axis=0, concat_axis=1, tiled=True),
        lax.all_to_all(decay_rate, "layer", split_axis=0, concat_axis=1, tiled=True),
        lax.all_to_all(facet_refl, "layer", split_axis=0, concat_axis=1, tiled=True),
    )
    block_index = lax.axis_index("blk")
    row_count = HARM // lax.axis_size("blk")
    row_start = block_index * row_count
    refl_full = relayed_refl.astype(jnp.float32)
    transmit = jnp.sqrt(1.0 - refl_full * refl_full) * jnp.exp(-relayed_decay.astype(jnp.float32))
    mode_piece = lax.all_gather(relayed_modes, "blk", axis=2, tiled=True)
    piece_wide = mode_piece.astype(jnp.float32)
    scaled_refl = (piece_wide * refl_full[:, None, :]).astype(jnp.bfloat16)
    scaled_tran = (piece_wide * transmit[:, None, :]).astype(jnp.bfloat16)
    own_rows = lax.dynamic_slice_in_dim(mode_piece, row_start, row_count, 1)
    refl_part = jnp.einsum(
        "lhm,lkm->lhk", own_rows, scaled_refl, preferred_element_type=jnp.float32
    )
    tran_part = jnp.einsum(
        "lhm,lkm->lhk", own_rows, scaled_tran, preferred_element_type=jnp.float32
    )
    refl_rows = refl_part.astype(jnp.bfloat16)
    tran_rows = tran_part.astype(jnp.bfloat16)
    layer_rows = jnp.stack([refl_rows, tran_rows, tran_rows, -refl_rows], axis=1)
    layer_pair = lax.all_gather(
        jnp.stack([refl_rows, tran_rows], axis=1), "blk", axis=2, tiled=True
    )
    rows_now = layer_rows[0]
    full_now = jnp.stack([layer_pair[0, 0], layer_pair[0, 1], layer_pair[0, 1], -layer_pair[0, 0]])
    rows_now = star_rows(rows_now[0:2], full_now[2:4], layer_pair[1], layer_rows[1, 2:4])
    full_now = lax.all_gather(rows_now, "blk", axis=1, tiled=True)
    group_index = lax.axis_index("layer")
    level_count = lax.axis_size("layer").bit_length() - 1
    for section_level in range(level_count):
        distance = 1 << section_level
        upper_whole = passed_along(full_now, "layer", distance)
        upper_near = lax.dynamic_slice_in_dim(upper_whole[0:2], row_start, row_count, 1)
        upper_far = upper_whole[2:4]
        combined = star_rows(upper_near, upper_far, full_now[0:2], rows_now[2:4])
        rows_now = jnp.where(group_index >= distance, combined, rows_now)
        if section_level + 1 < level_count:
            full_now = lax.all_gather(rows_now, "blk", axis=1, tiled=True)
    return rows_now[None]


def solution(mesh):
    placed = (P(None, "layer", "blk"), P(None, "layer"), P(None, "layer"))
    return jax.shard_map(
        on_device,
        mesh=mesh,
        in_specs=placed,
        out_specs=P("layer", None, "blk", None),
        check_vma=False,
    )
```

profile of v0, /device:TPU:28, one launch (start us, length us, event | category | flops | bytes accessed | tf_op | source)
XLA Modules:
  0.0 381.9 jit_solution(7659137016410913548)
XLA Ops:
  6.5 12.5 %all_to_all.44 = bf16[16,64,128]{2,1,0:T(8,128)(2,1)S(1)} all-to-all(bf16[16,64,128]{2,1,0:T(8,128)(2,1)} %param.3), channel_id=1, replica_groups=mesh['layer'=8,'blk'=4] {'layer'}, dimensions={0} | all-to-all | bytes 524288 | tf_op jit(solution)/shard_map/all_to_all | solution.py:40
  19.8 6.0 %all-to-all-start.2 = ((bf16[8,2,64]{2,1,0:T(2,128)(2,1)}), bf16[8,2,64]{2,1,0:T(2,128)(2,1)S(1)}, u32[]{:S(2)}, u32[]{:S(2)}) async-start(bf16[8,2,64]{2,1,0:T(2,128)(2,1)} %bitcast.380), calls=%async_computation.2 | async-start | bytes 8192 | tf_op jit(solution)/shard_map/all_to_all | solution.py:41
  25.8 2.2 all-to-all-done.2
  28.0 7.4 %all-to-all-start.1 = ((bf16[8,2,64]{2,1,0:T(2,128)(2,1)}), bf16[8,2,64]{2,1,0:T(2,128)(2,1)S(1)}, u32[]{:S(2)}, u32[]{:S(2)}) async-start(bf16[8,2,64]{2,1,0:T(2,128)(2,1)} %bitcast.381), calls=%async_computation.1 | async-start | bytes 8192 | tf_op jit(solution)/shard_map/all_to_all | solution.py:42
  35.5 2.1 all-to-all-done.1
  37.8 1.8 convolution_convert_fusion.9
  39.6 1.8 convolution_convert_fusion.8
  42.3 23.7 %all-gather.8.cloned.1.call-done = bf16[2,2,512,512]{3,2,0,1:T(8,128)(2,1)} async-done(((bf16[2,2,128,512]{3,2,0,1:T(8,128)(2,1)}), bf16[2,2,512,512]{3,2,0,1:T(8,128)(2,1)}) %all-gather.8.cloned.1.call-update) | async-done | bytes 2097168 | tf_op jit(solution)/shard_map/all_gather | solution.py:63
  66.0 1.8 convolution_convert_fusion.6
  72.1 22.7 %all-gather.10.cloned.1.call-done = bf16[4,512,512]{2,1,0:T(8,128)(2,1)} async-done(((bf16[4,128,512]{2,1,0:T(8,128)(2,1)}), bf16[4,512,512]{2,1,0:T(8,128)(2,1)}) %all-gather.10.cloned.1.call-update) | async-done | bytes 2097168 | tf_op jit(solution)/shard_map/all_gather | solution.py:69
  96.1 48.7 %collective-permute-done = bf16[4,512,512]{2,1,0:T(8,128)(2,1)} collective-permute-done((bf16[4,512,512]{2,1,0:T(8,128)(2,1)}, bf16[4,512,512]{2,1,0:T(8,128)(2,1)}, u32[]{:S(2)}, u32[]{:S(2)}) %collective-permute-start) | collective-permute-done | bytes 2097184 | tf_op jit(solution)/shard_map/ppermute | solution.py:13
  144.8 1.6 convolution_convert_fusion.4
  147.2 1.6 convolution_convert_fusion.5
  148.9 1.3 slice.250
  151.0 1.6 fusion.12
  153.9 1.6 fusion.72
  157.8 22.7 %all-gather.12.cloned.1.call-done = bf16[4,512,512]{2,1,0:T(8,128)(2,1)} async-done(((bf16[4,128,512]{2,1,0:T(8,128)(2,1)}), bf16[4,512,512]{2,1,0:T(8,128)(2,1)}) %all-gather.12.cloned.1.call-update) | async-done | bytes 2097168 | tf_op jit(solution)/shard_map/all_gather | solution.py:80
  181.8 48.7 %collective-permute-done.1 = bf16[4,512,512]{2,1,0:T(8,128)(2,1)} collective-permute-done((bf16[4,512,512]{2,1,0:T(8,128)(2,1)}, bf16[4,512,512]{2,1,0:T(8,128)(2,1)}, u32[]{:S(2)}, u32[]{:S(2)}) %collective-permute-start.1) | collective-permute-done | bytes 2097184 | tf_op jit(solution)/shard_map/ppermute | solution.py:13
  230.5 1.6 convolution_convert_fusion.2
  232.9 1.6 convolution_convert_fusion.3
  234.6 1.3 slice.255
  236.7 1.6 fusion.17
  238.3 1.3 convolution_convert_fusion.15
  239.6 1.7 fusion.71
  241.3 1.3 convolution_convert_fusion.16
  243.7 22.7 %all-gather.14.cloned.1.call-done = bf16[4,512,512]{2,1,0:T(8,128)(2,1)} async-done(((bf16[4,128,512]{2,1,0:T(8,128)(2,1)}), bf16[4,512,512]{2,1,0:T(8,128)(2,1)}) %all-gather.14.cloned.1.call-update) | async-done | bytes 2097168 | tf_op jit(solution)/shard_map/all_gather | solution.py:80
  267.7 94.5 %collective-permute-done.2 = bf16[4,512,512]{2,1,0:T(8,128)(2,1)} collective-permute-done((bf16[4,512,512]{2,1,0:T(8,128)(2,1)}, bf16[4,512,512]{2,1,0:T(8,128)(2,1)}, u32[]{:S(2)}, u32[]{:S(2)}) %collective-permute-start.2) | collective-permute-done | bytes 2097184 | tf_op jit(solution)/shard_map/ppermute | solution.py:13
  362.2 1.6 convolution_convert_fusion
  364.7 1.6 convolution_convert_fusion.1
  366.3 1.3 slice.262
  368.5 1.7 fusion.41
  371.4 1.6 fusion.75
  (74 shorter events, 22.9 us)
Async XLA Ops:
  6.5 31.2 %all-gather.6.cloned.1.call-start = ((), (), s32[]{:S(2)}) async-start(), calls=%async_computation.3 | async-start | bytes 1310720 | tf_op jit(solution)/shard_map/all_gather | solution.py:49
  19.8 8.3 %all-to-all-start.2 = ((bf16[8,2,64]{2,1,0:T(2,128)(2,1)}), bf16[8,2,64]{2,1,0:T(2,128)(2,1)S(1)}, u32[]{:S(2)}, u32[]{:S(2)}) async-start(bf16[8,2,64]{2,1,0:T(2,128)(2,1)} %bitcast.380), calls=%async_computation.2 | async-start | bytes 8192 | tf_op jit(solution)/shard_map/all_to_all | solution.py:41
  28.0 9.6 %all-to-all-start.1 = ((bf16[8,2,64]{2,1,0:T(2,128)(2,1)}), bf16[8,2,64]{2,1,0:T(2,128)(2,1)S(1)}, u32[]{:S(2)}, u32[]{:S(2)}) async-start(bf16[8,2,64]{2,1,0:T(2,128)(2,1)} %bitcast.381), calls=%async_computation.1 | async-start | bytes 8192 | tf_op jit(solution)/shard_map/all_to_all | solution.py:42
  35.4 30.5 %all-gather.8.cloned.1.call-start = ((), (), s32[]{:S(2)}) async-start(), calls=%async_computation.4 | async-start | bytes 2621440 | tf_op jit(solution)/shard_map/all_gather | solution.py:63
  42.3 52.5 %all-gather.10.cloned.1.call-start = ((), (), s32[]{:S(2)}) async-start(), calls=%async_computation.5 | async-start | bytes 2621440 | tf_op jit(solution)/shard_map/all_gather | solution.py:69
  66.0 2.6 copy-start.10
  72.1 108.4 %all-gather.12.cloned.1.call-start = ((), (), s32[]{:S(2)}) async-start(), calls=%async_computation.6 | async-start | bytes 2621440 | tf_op jit(solution)/shard_map/all_gather | solution.py:80
  94.8 50.0 %collective-permute-start = (bf16[4,512,512]{2,1,0:T(8,128)(2,1)}, bf16[4,512,512]{2,1,0:T(8,128)(2,1)}, u32[]{:S(2)}, u32[]{:S(2)}) collective-permute-start(bf16[4,512,512]{2,1,0:T(8,128)(2,1)} %all-gather.10.cloned.1.call-done), channel_id=1, source_target_pairs={{0,4},{4,8},{8,12},{12,16},{16,20},{20,24},{24,28},{1,5},{5,9},{9,... | collective-permute-start | bytes 6291464 | tf_op jit(solution)/shard_map/ppermute | solution.py:13
  157.7 74.4 %copy-start = (bf16[4,128,512]{2,1,0:T(8,128)(2,1)S(1)}, bf16[4,128,512]{2,1,0:T(8,128)(2,1)}, u32[]{:S(2)}) copy-start(bf16[4,128,512]{2,1,0:T(8,128)(2,1)} %maximum_select_fusion) | copy-start | bytes 1572868
  157.7 108.7 %all-gather.14.cloned.1.call-start = ((), (), s32[]{:S(2)}) async-start(), calls=%async_computation.7 | async-start | bytes 2621440 | tf_op jit(solution)/shard_map/all_gather | solution.py:80
  180.5 50.0 %collective-permute-start.1 = (bf16[4,512,512]{2,1,0:T(8,128)(2,1)}, bf16[4,512,512]{2,1,0:T(8,128)(2,1)}, u32[]{:S(2)}, u32[]{:S(2)}) collective-permute-start(bf16[4,512,512]{2,1,0:T(8,128)(2,1)} %all-gather.12.cloned.1.call-done), channel_id=1, source_target_pairs={{0,8},{4,12},{8,16},{12,20},{16,24},{20,28},{1,9},{5,13},{9,17},{1... | collective-permute-start | bytes 6291464 | tf_op jit(solution)/shard_map/ppermute | solution.py:13
  238.3 5.3 %copy-start.2 = (bf16[128,512]{1,0:T(8,128)(2,1)}, bf16[128,512]{1,0:T(8,128)(2,1)S(1)}, u32[]{:S(2)}) copy-start(bf16[128,512]{1,0:T(8,128)(2,1)S(1)} %fusion.17) | copy-start | bytes 393220
  239.6 4.0 %copy-start.4 = (bf16[128,512]{1,0:T(8,128)(2,1)}, bf16[128,512]{1,0:T(8,128)(2,1)S(1)}, u32[]{:S(2)}) copy-start(bf16[128,512]{1,0:T(8,128)(2,1)S(1)} %convolution_convert_fusion.15) | copy-start | bytes 393220
  241.3 26.4 %copy-start.6 = (bf16[128,512]{1,0:T(8,128)(2,1)}, bf16[128,512]{1,0:T(8,128)(2,1)S(1)}, u32[]{:S(2)}) copy-start(bf16[128,512]{1,0:T(8,128)(2,1)S(1)} %fusion.71) | copy-start | bytes 393220
  242.6 25.1 %copy-start.8 = (bf16[128,512]{1,0:T(8,128)(2,1)}, bf16[128,512]{1,0:T(8,128)(2,1)S(1)}, u32[]{:S(2)}) copy-start(bf16[128,512]{1,0:T(8,128)(2,1)S(1)} %convolution_convert_fusion.16) | copy-start | bytes 393220
  243.6 120.2 %copy-start.1 = (bf16[4,128,512]{2,1,0:T(8,128)(2,1)S(1)}, bf16[4,128,512]{2,1,0:T(8,128)(2,1)}, u32[]{:S(2)}) copy-start(bf16[4,128,512]{2,1,0:T(8,128)(2,1)} %maximum_select_fusion.1) | copy-start | bytes 1572868
  266.4 95.8 %collective-permute-start.2 = (bf16[4,512,512]{2,1,0:T(8,128)(2,1)}, bf16[4,512,512]{2,1,0:T(8,128)(2,1)}, u32[]{:S(2)}, u32[]{:S(2)}) collective-permute-start(bf16[4,512,512]{2,1,0:T(8,128)(2,1)} %all-gather.14.cloned.1.call-done), channel_id=1, source_target_pairs={{0,16},{4,20},{8,24},{12,28},{1,17},{5,21},{9,25},{13,29},{2,18},{... | collective-permute-start | bytes 6291464 | tf_op jit(solution)/shard_map/ppermute | solution.py:13
  368.4 5.9 %copy-start.3 = (bf16[128,512]{1,0:T(8,128)(2,1)S(1)}, bf16[128,512]{1,0:T(8,128)(2,1)}, u32[]{:S(2)}) copy-start(bf16[128,512]{1,0:T(8,128)(2,1)} %copy-done.2) | copy-start | bytes 393220
  368.4 5.9 %copy-start.5 = (bf16[128,512]{1,0:T(8,128)(2,1)S(1)}, bf16[128,512]{1,0:T(8,128)(2,1)}, u32[]{:S(2)}) copy-start(bf16[128,512]{1,0:T(8,128)(2,1)} %copy-done.4) | copy-start | bytes 393220
  368.5 5.9 %copy-start.7 = (bf16[128,512]{1,0:T(8,128)(2,1)S(1)}, bf16[128,512]{1,0:T(8,128)(2,1)}, u32[]{:S(2)}) copy-start(bf16[128,512]{1,0:T(8,128)(2,1)} %copy-done.6) | copy-start | bytes 393220
  368.5 5.9 %copy-start.9 = (bf16[128,512]{1,0:T(8,128)(2,1)S(1)}, bf16[128,512]{1,0:T(8,128)(2,1)}, u32[]{:S(2)}) copy-start(bf16[128,512]{1,0:T(8,128)(2,1)} %copy-done.8) | copy-start | bytes 393220
Sparse Core Ops, SparseCore 0:
  19.9 17.7 all-gather.5
  42.4 23.5 all-gather.7
  72.2 22.5 all-gather.9
  157.9 22.5 all-gather.11
  243.8 22.5 all-gather.13
where the time goes:
time: 383 us; the launch traced here: 382 us
  waiting for transfers between devices  288 us (75%)
  matrix products  40.8 us (11%)
  starting transfers between devices  17.4 us (5%)
  between operations  13.7 us (4%)
  blocking collectives  12.5 us (3%)
  local copies, waits for them, and re-layouts  4.81 us (1%)
  other arithmetic  4.68 us (1%)
    ppermute x3, waiting for transfers between devices, passed_along(): lax.ppermute(value, axis, [(source, source + steps) for source in range(f...  192 us
    all_gather x3, waiting for transfers between devices, on_device(): full_now = lax.all_gather(rows_now, 'blk', axis=1, tiled=True)  68.1 us
    dot_general x40, matrix products, times_f32(): return jnp.dot(left_op, right_op, preferred_element_type=jnp.float32)  37.2 us
    all_gather x1, waiting for transfers between devices, on_device(): lax.all_gather(jnp.stack([refl_rows, tran_rows], axis=1), 'blk', axis=2,...  23.7 us
    all_to_all x1, blocking collectives, on_device(): lax.all_to_all(mode_matrix, 'layer', split_axis=0, concat_axis=1, tiled=T...  12.5 us
  transfers between devices with their start and end apart: 10, of which 9 were waited for; matrix products, arithmetic and copies ran while one was open for 0% of the time, Pallas kernels for 0%

commit v1 on v0

v1 whole, which is shorter than its diff:
```python
import functools

import jax
import jax.numpy as jnp
from jax import lax
from jax.experimental import pallas as pl
from jax.experimental.pallas import tpu as pltpu
from jax.sharding import PartitionSpec as P

REFL = 4
LANES = 128
MESH = pl.DeviceIdType.MESH


def dot(left_op, right_op):
    return jnp.dot(left_op, right_op, preferred_element_type=jnp.float32)


def stack_kernel(
    n, nb, levels,
    mode_ref, aux_ref, out_ref,
    mrecv, arecv, modes, scaled, layer_s, state, land,
    down, up, left, right, mid,
    mode_send, mode_recv, aux_send, aux_recv, share_send, share_recv,
    far_send, far_recv, relay_send, relay_recv,
):
    group = lax.axis_index("layer")
    blk = lax.axis_index("blk")
    cross = lax.rem(blk + 2, nb)
    sib = blk + 1 - 2 * lax.rem(blk, 2)
    sib_cross = lax.rem(sib + 2, nb)
    harm = state.shape[-1]
    rows = harm // nb
    lay = mode_ref.shape[0] // n
    mode_local = harm // n

    def block_rows(index):
        return pl.ds(pl.multiple_of(index * rows, rows), rows)

    own = block_rows(blk)

    barrier = pltpu.get_barrier_semaphore()

    def greet(offset, carry):
        pl.semaphore_signal(
            barrier, inc=1, device_id=(lax.rem(group + offset, n), blk), device_id_type=MESH
        )
        return carry

    lax.fori_loop(1, n, greet, 0)
    for other in (cross, sib):
        pl.semaphore_signal(barrier, inc=1, device_id=(group, other), device_id_type=MESH)
    pl.semaphore_wait(barrier, n + 1)

    def mode_copy(offset):
        target = lax.rem(group + offset, n)
        return pltpu.make_async_remote_copy(
            src_ref=mode_ref.at[pl.ds(target * lay, lay)],
            dst_ref=mrecv.at[blk, group],
            send_sem=mode_send.at[offset],
            recv_sem=mode_recv.at[offset],
            device_id=(target, blk),
            device_id_type=MESH,
        )

    def aux_copy(offset):
        target = lax.rem(group + offset, n)
        return pltpu.make_async_remote_copy(
            src_ref=aux_ref.at[target],
            dst_ref=arecv.at[group],
            send_sem=aux_send.at[offset],
            recv_sem=aux_recv.at[offset],
            device_id=(target, blk),
            device_id_type=MESH,
        )

    def start_modes(offset, carry):
        mode_copy(offset).start()
        aux_copy(offset).start()
        return carry

    lax.fori_loop(1, n, start_modes, 0)
    mrecv[blk, group] = mode_ref[pl.ds(group * lay, lay)]
    arecv[group] = aux_ref[group]

    def end_modes(offset, carry):
        mode_copy(offset).wait_recv()
        aux_copy(offset).wait_recv()
        return carry

    lax.fori_loop(1, n, end_modes, 0)

    def share_copy(index, piece, other):
        return pltpu.make_async_remote_copy(
            src_ref=mrecv.at[piece],
            dst_ref=mrecv.at[piece],
            send_sem=share_send.at[index],
            recv_sem=share_recv.at[index],
            device_id=(group, other),
            device_id_type=MESH,
        )

    share_copy(0, blk, cross).start()
    share_copy(1, blk, sib).start()
    share_copy(0, cross, cross).wait_recv()
    share_copy(2, cross, sib).start()
    share_copy(1, sib, sib).wait_recv()
    share_copy(2, sib_cross, sib).wait_recv()

    per_window = LANES // mode_local
    windows = [
        sum(arecv[index] for index in range(w * per_window, (w + 1) * per_window))
        for w in range(harm // LANES)
    ]
    for layer in range(lay):
        for piece in range(nb):
            cols = slice(piece * rows, (piece + 1) * rows)
            wide = mrecv[piece, :, layer].astype(jnp.float32).reshape(harm, rows)
            modes[:, cols] = wide.astype(jnp.bfloat16)
            coeff = windows[piece]
            scaled[0, :, cols] = (wide * coeff[lay + layer][None]).astype(jnp.bfloat16)
            scaled[1, :, cols] = (wide * coeff[layer][None]).astype(jnp.bfloat16)
        for kind in range(2):
            layer_s[layer, kind] = lax.dot_general(
                modes[...], scaled[kind], (((1,), (1,)), ((), ())),
                preferred_element_type=jnp.float32,
            ).astype(jnp.bfloat16)
        layer_s[layer, 2] = -layer_s[layer, 0]

    def far_copy(level, distance, slot, part):
        return pltpu.make_async_remote_copy(
            src_ref=state.at[slot, part, own],
            dst_ref=land.at[level, part, own],
            send_sem=far_send.at[level, part],
            recv_sem=far_recv.at[level, part],
            device_id=(lax.rem(group + distance, n), blk),
            device_id_type=MESH,
        )

    def send_far(level, distance, slot, part):
        @pl.when(group + distance < n)
        def _():
            far_copy(level, distance, slot, part).start()

    def relay_copy(level, part, index, piece, other):
        where = land.at[level, part, block_rows(piece)]
        return pltpu.make_async_remote_copy(
            src_ref=where,
            dst_ref=where,
            send_sem=relay_send.at[level, part, index],
            recv_sem=relay_recv.at[level, part, index],
            device_id=(group, other),
            device_id_type=MESH,
        )

    def relay_first(level, part):
        far_copy(level, 1, 0, part).wait_recv()
        relay_copy(level, part, 0, blk, cross).start()
        relay_copy(level, part, 1, blk, sib).start()

    def relay_second(level, part):
        relay_copy(level, part, 0, cross, cross).wait_recv()
        relay_copy(level, part, 2, cross, sib).start()

    def relay_end(level, part):
        relay_copy(level, part, 1, sib, sib).wait_recv()
        relay_copy(level, part, 2, sib_cross, sib).wait_recv()

    def chain(total, start, coupling, repeats, first):
        for repeat in range(repeats):
            source = start if first and repeat == 0 else total
            total[...] = (start[...] + dot(source[...], coupling[...])).astype(jnp.bfloat16)

    def full_star(a11, a12, a21, a22, b11, b12, b21, b22, into, send, hooks):
        hooks[0]()
        up[...] = dot(a22[...], b11[...]).astype(jnp.bfloat16)
        chain(right, b21, up, 2, True)
        hooks[1]()
        chain(right, b21, up, 2, False)
        mid[...] = dot(right[...], a22[...]).astype(jnp.bfloat16)
        into[3] = (b22[...] + dot(mid[...], b12[...])).astype(jnp.bfloat16)
        send(3)
        down[...] = dot(b11[...], a22[...]).astype(jnp.bfloat16)
        hooks[2]()
        chain(left, a12, down, REFL, True)
        into[1] = dot(left[...], b12[...]).astype(jnp.bfloat16)
        send(1)
        hooks[3]()
        into[2] = dot(right[...], a21[...]).astype(jnp.bfloat16)
        send(2)
        mid[...] = dot(left[...], b11[...]).astype(jnp.bfloat16)
        hooks[4]()
        into[0] = (a11[...] + dot(mid[...], a21[...])).astype(jnp.bfloat16)
        send(0)

    def parts(ref):
        return [ref.at[part] for part in range(4)]

    def layer_parts(layer):
        refl, tran, back = [layer_s.at[layer, kind] for kind in range(3)]
        return [refl, tran, tran, back]

    nothing = [lambda: None] * 5
    last = levels - 1
    assert lay == 2
    full_star(
        *layer_parts(0), *layer_parts(1), state.at[0],
        lambda part: send_far(0, 1, 0, part), nothing,
    )

    slot_end = sum(jnp.where(group >= (1 << k), 1, 0) for k in range(last))

    def one_level(level, distance):
        @pl.when(group >= distance)
        def _():
            def hook0():
                relay_first(level, 3)
                relay_first(level, 1)
                relay_second(level, 3)
                relay_end(level, 3)

            def hook1():
                relay_first(level, 2)
                relay_second(level, 1)

            def hook2():
                relay_end(level, 1)
                relay_first(level, 0)
                relay_second(level, 2)

            def hook3():
                relay_end(level, 2)
                relay_second(level, 0)

            def hook4():
                relay_end(level, 0)

            full_star(
                *parts(land.at[level]), *parts(state.at[level]), state.at[level + 1],
                lambda part: send_far(level + 1, 2 * distance, level + 1, part),
                [hook0, hook1, hook2, hook3, hook4],
            )

        @pl.when(group < distance)
        def _():
            for part in (3, 1, 2, 0):
                send_far(level + 1, 2 * distance, slot_end, part)

        return 2 * distance

    lax.fori_loop(0, last, one_level, 1)

    half = 1 << last

    @pl.when(group < half)
    def _():
        out_ref[...] = state[slot_end, :, own]

    @pl.when(group >= half)
    def _():
        a11, a12, a21, a22 = parts(land.at[last])
        b11, b12, b21, b22 = parts(state.at[last])
        right_rows, left_rows = right.at[:rows], left.at[:rows]
        relay_first(last, 3)
        relay_second(last, 3)
        relay_end(last, 3)
        up[...] = dot(a22[...], b11[...]).astype(jnp.bfloat16)
        down[...] = dot(b11[...], a22[...]).astype(jnp.bfloat16)
        far_copy(last, 1, 0, 1).wait_recv()
        relay_first(last, 2)
        chain(right_rows, b21.at[own], up, REFL, True)
        chain(left_rows, a12.at[own], down, REFL, True)
        right_mid = dot(right_rows[...], a22[...]).astype(jnp.bfloat16)
        left_mid = dot(left_rows[...], b11[...]).astype(jnp.bfloat16)
        out_ref[1] = dot(left_rows[...], b12[...]).astype(jnp.bfloat16)
        out_ref[3] = (b22[own] + dot(right_mid, b12[...])).astype(jnp.bfloat16)
        relay_second(last, 2)
        relay_end(last, 2)
        out_ref[2] = dot(right_rows[...], a21[...]).astype(jnp.bfloat16)
        far_copy(last, 1, 0, 0).wait_recv()
        out_ref[0] = (a11[own] + dot(left_mid, a21[...])).astype(jnp.bfloat16)

    def leave_modes(offset, carry):
        mode_copy(offset).wait_send()
        aux_copy(offset).wait_send()
        return carry

    lax.fori_loop(1, n, leave_modes, 0)
    share_copy(0, blk, cross).wait_send()
    share_copy(1, blk, sib).wait_send()
    share_copy(2, cross, sib).wait_send()
    for level in range(levels):
        @pl.when(group + (1 << level) < n)
        def _(level=level):
            for part in range(4):
                far_copy(level, 1, 0, part).wait_send()

        @pl.when(group >= (1 << level))
        def _(level=level):
            for part in range(4) if level < last else (2, 3):
                relay_copy(level, part, 0, blk, cross).wait_send()
                relay_copy(level, part, 1, blk, sib).wait_send()
                relay_copy(level, part, 2, cross, sib).wait_send()


def on_device(n, nb, mode_matrix, decay_rate, facet_refl):
    layers, mode_local = decay_rate.shape
    harm = n * mode_matrix.shape[1]
    lay = layers // n
    levels = n.bit_length() - 1
    refl = facet_refl.astype(jnp.float32)
    tran = jnp.sqrt(1.0 - refl * refl) * jnp.exp(-decay_rate.astype(jnp.float32))
    coeff = jnp.concatenate(
        [tran.reshape(n, lay, mode_local), refl.reshape(n, lay, mode_local)], axis=1
    )
    coeff = jnp.pad(coeff, ((0, 0), (0, 8 - 2 * lay), (0, 0)))
    copies = LANES // mode_local
    place = lax.broadcasted_iota(jnp.int32, (1, 1, LANES), 2) // mode_local
    aux = jnp.where(
        place == lax.rem(lax.axis_index("layer"), copies), jnp.tile(coeff, (1, 1, copies)), 0.0
    )
    square = (harm, harm)
    dma = pltpu.SemaphoreType.DMA
    vmem = pl.BlockSpec(memory_space=pltpu.VMEM)
    result = pl.pallas_call(
        functools.partial(stack_kernel, n, nb, levels),
        out_shape=jax.ShapeDtypeStruct((4, harm // nb, harm), jnp.bfloat16),
        in_specs=[vmem, vmem],
        out_specs=vmem,
        scratch_shapes=[
            pltpu.VMEM((nb, n, lay) + mode_matrix.shape[1:], jnp.bfloat16),
            pltpu.VMEM((n, 8, LANES), jnp.float32),
            pltpu.VMEM(square, jnp.bfloat16),
            pltpu.VMEM((2,) + square, jnp.bfloat16),
            pltpu.VMEM((lay, 3) + square, jnp.bfloat16),
            pltpu.VMEM((levels, 4) + square, jnp.bfloat16),
            pltpu.VMEM((levels, 4) + square, jnp.bfloat16),
        ]
        + [pltpu.VMEM(square, jnp.bfloat16)] * 5
        + [dma((n,))] * 4
        + [dma((3,))] * 2
        + [dma((levels, 4))] * 2
        + [dma((levels, 4, 3))] * 2,
        compiler_params=pltpu.CompilerParams(
            collective_id=0, has_side_effects=True, vmem_limit_bytes=56 * 1024 * 1024
        ),
        cost_estimate=pl.CostEstimate(
            flops=2 * harm**3 * 60, bytes_accessed=2**20, transcendentals=0
        ),
    )(mode_matrix, aux)
    return result[None]


def solution(mesh):
    n, nb = mesh.shape["layer"], mesh.shape["blk"]
    placed = (P(None, "layer", "blk"), P(None, "layer"), P(None, "layer"))
    return jax.shard_map(
        functools.partial(on_device, n, nb),
        mesh=mesh,
        in_specs=placed,
        out_specs=P("layer", None, "blk", None),
        check_vma=False,
    )
```

time: 383 us -> 87 us (0.23)
  the two profiles are of different devices: /device:TPU:28 before, /device:TPU:17 now
where the time goes in v1:
time: 87 us; the launch traced here: 86.7 us
  Pallas kernels  83.4 us (96%)
  local copies, waits for them, and re-layouts  2.69 us (3%)
    pallas_call x1, Pallas kernels, on_device(): pl.pallas_call(functools.partial(stack_kernel, n, nb, levels), out_shape=...  83.4 us
    unnamed x5, local copies, waits for them, and re-layouts  2.56 us

profile of v1, /device:TPU:17, one launch (start us, length us, event | category | flops | bytes accessed | tf_op | source)
XLA Modules:
  0.0 86.7 jit_solution(14455297968534467070)
XLA Ops:
  0.0 0.0 copy-start.1
  0.0 0.0 copy-start
  0.0 0.7 copy-done.1
  0.7 0.0 copy-done
  0.8 0.1 tile.10
  0.9 0.6 broadcast_select_fusion.aux_ref
  1.5 83.4 %shard_map.37 = bf16[4,128,512]{2,1,0:T(8,128)(2,1)} custom-call(bf16[16,64,128]{2,1,0:T(8,128)(2,1)} %mode_ref.1, f32[8,8,128]{2,1,0:T(8,128)} %broadcast_select_fusion.aux_ref), custom_call_target="tpu_custom_call" | custom-call | flops 16106127360 | bytes 1048576 | tf_op jit(solution)/shard_map/pallas_call | solution.py:325
  84.9 1.9 %copy.5 = bf16[1,4,128,512]{3,2,1,0:T(8,128)(2,1)} copy(bf16[1,4,128,512]{3,2,1,0:T(8,128)(2,1)} %bitcast.4) | data formatting | bytes 1048576
  (5 shorter events, 0.1 us)
Async XLA Ops:
  0.0 0.7 copy-start.1
  0.0 0.7 copy-start

commit v2 on v1

v2 whole, which is shorter than its diff:
```python
import functools

import jax
import jax.numpy as jnp
from jax import lax
from jax.experimental import pallas as pl
from jax.experimental.pallas import tpu as pltpu
from jax.sharding import PartitionSpec as P

REFL = 4
LANES = 128
HALVES = 2
MESH = pl.DeviceIdType.MESH


def dot(left_op, right_op):
    return jnp.dot(left_op, right_op, preferred_element_type=jnp.float32)


def stack_kernel(
    n, nb, levels,
    mode_ref, aux_ref, out_ref,
    mrecv, arecv, modes, scaled, layer_s, state, land,
    down, up, left, right, mid,
    mode_send, mode_recv, aux_send, aux_recv, share_send, share_recv,
    far_send, far_recv, relay_send, relay_recv,
):
    group = lax.axis_index("layer")
    blk = lax.axis_index("blk")
    cross = lax.rem(blk + 2, nb)
    sib = blk + 1 - 2 * lax.rem(blk, 2)
    sib_cross = lax.rem(sib + 2, nb)
    harm = state.shape[-1]
    rows = harm // nb
    lay = mode_ref.shape[0] // n
    mode_local = harm // n

    def block_rows(index):
        return pl.ds(pl.multiple_of(index * rows, rows), rows)

    own = block_rows(blk)

    barrier = pltpu.get_barrier_semaphore()

    def greet(offset, carry):
        pl.semaphore_signal(
            barrier, inc=1, device_id=(lax.rem(group + offset, n), blk), device_id_type=MESH
        )
        return carry

    lax.fori_loop(1, n, greet, 0)
    for other in (cross, sib):
        pl.semaphore_signal(barrier, inc=1, device_id=(group, other), device_id_type=MESH)
    pl.semaphore_wait(barrier, n + 1)

    def mode_copy(offset, layer):
        target = lax.rem(group + offset, n)
        return pltpu.make_async_remote_copy(
            src_ref=mode_ref.at[target * lay + layer],
            dst_ref=mrecv.at[blk, layer, group],
            send_sem=mode_send.at[offset, layer],
            recv_sem=mode_recv.at[offset, layer],
            device_id=(target, blk),
            device_id_type=MESH,
        )

    def aux_copy(offset):
        target = lax.rem(group + offset, n)
        return pltpu.make_async_remote_copy(
            src_ref=aux_ref.at[target],
            dst_ref=arecv.at[group],
            send_sem=aux_send.at[offset],
            recv_sem=aux_recv.at[offset],
            device_id=(target, blk),
            device_id_type=MESH,
        )

    def for_offsets(body):
        def step(offset, carry):
            body(offset)
            return carry

        lax.fori_loop(1, n, step, 0)

    for layer in range(lay):
        for_offsets(lambda offset: mode_copy(offset, layer).start())
        if layer == 0:
            for_offsets(lambda offset: aux_copy(offset).start())
        mrecv[blk, layer, group] = mode_ref[group * lay + layer]
    arecv[group] = aux_ref[group]

    def share_copy(layer, index, piece, other):
        return pltpu.make_async_remote_copy(
            src_ref=mrecv.at[piece, layer],
            dst_ref=mrecv.at[piece, layer],
            send_sem=share_send.at[layer, index],
            recv_sem=share_recv.at[layer, index],
            device_id=(group, other),
            device_id_type=MESH,
        )

    for layer in range(lay):
        for_offsets(lambda offset: mode_copy(offset, layer).wait_recv())
        share_copy(layer, 0, blk, cross).start()
        share_copy(layer, 1, blk, sib).start()
    for_offsets(lambda offset: aux_copy(offset).wait_recv())
    per_window = LANES // mode_local
    windows = [
        sum(arecv[index] for index in range(w * per_window, (w + 1) * per_window))
        for w in range(harm // LANES)
    ]

    for layer in range(lay):
        share_copy(layer, 0, cross, cross).wait_recv()
        share_copy(layer, 2, cross, sib).start()
        share_copy(layer, 1, sib, sib).wait_recv()
        share_copy(layer, 2, sib_cross, sib).wait_recv()
        for piece in range(nb):
            cols = slice(piece * rows, (piece + 1) * rows)
            wide = mrecv[piece, layer].astype(jnp.float32).reshape(harm, rows)
            modes[:, cols] = wide.astype(jnp.bfloat16)
            coeff = windows[piece]
            scaled[0, :, cols] = (wide * coeff[lay + layer][None]).astype(jnp.bfloat16)
            scaled[1, :, cols] = (wide * coeff[layer][None]).astype(jnp.bfloat16)
        for kind in range(2):
            layer_s[layer, kind] = lax.dot_general(
                modes[...], scaled[kind], (((1,), (1,)), ((), ())),
                preferred_element_type=jnp.float32,
            ).astype(jnp.bfloat16)
        layer_s[layer, 2] = -layer_s[layer, 0]

    def piece_rows(index, half):
        size = rows // HALVES
        return pl.ds(pl.multiple_of(index * rows + half * size, size), size)

    def far_copy(level, distance, slot, part, half):
        return pltpu.make_async_remote_copy(
            src_ref=state.at[slot, part, piece_rows(blk, half)],
            dst_ref=land.at[level, part, piece_rows(blk, half)],
            send_sem=far_send.at[level, part, half],
            recv_sem=far_recv.at[level, part, half],
            device_id=(lax.rem(group + distance, n), blk),
            device_id_type=MESH,
        )

    def send_far(level, distance, slot, part):
        @pl.when(group + distance < n)
        def _():
            for half in range(HALVES):
                far_copy(level, distance, slot, part, half).start()

    def far_left(level):
        for part in range(4):
            for half in range(HALVES):
                far_copy(level, 1, 0, part, half).wait_send()

    def relay_copy(level, part, half, index, piece, other):
        where = land.at[level, part, piece_rows(piece, half)]
        return pltpu.make_async_remote_copy(
            src_ref=where,
            dst_ref=where,
            send_sem=relay_send.at[level, part, half, index],
            recv_sem=relay_recv.at[level, part, half, index],
            device_id=(group, other),
            device_id_type=MESH,
        )

    def relay_first(level, part, half):
        far_copy(level, 1, 0, part, half).wait_recv()
        relay_copy(level, part, half, 0, blk, cross).start()
        relay_copy(level, part, half, 1, blk, sib).start()

    def relay_second(level, part, half):
        relay_copy(level, part, half, 0, cross, cross).wait_recv()
        relay_copy(level, part, half, 2, cross, sib).start()

    def relay_end(level, part):
        for half in range(HALVES):
            relay_copy(level, part, half, 1, sib, sib).wait_recv()
            relay_copy(level, part, half, 2, sib_cross, sib).wait_recv()

    def chain(total, start, coupling, repeat):
        source = start if repeat == 0 else total
        total[...] = (start[...] + dot(source[...], coupling[...])).astype(jnp.bfloat16)

    def full_star(a11, a12, a21, a22, b11, b12, b21, b22, into, send, first, second, end):
        first(3, 0)
        first(3, 1)
        second(3, 0)
        first(1, 0)
        second(3, 1)
        end(3)
        up[...] = dot(a22[...], b11[...]).astype(jnp.bfloat16)
        first(1, 1)
        chain(right, b21, up, 0)
        second(1, 0)
        chain(right, b21, up, 1)
        chain(right, b21, up, 2)
        second(1, 1)
        chain(right, b21, up, 3)
        mid[...] = dot(right[...], a22[...]).astype(jnp.bfloat16)
        into[3] = (b22[...] + dot(mid[...], b12[...])).astype(jnp.bfloat16)
        send(3)
        first(2, 0)
        down[...] = dot(b11[...], a22[...]).astype(jnp.bfloat16)
        first(2, 1)
        end(1)
        chain(left, a12, down, 0)
        second(2, 0)
        first(0, 0)
        chain(left, a12, down, 1)
        second(2, 1)
        first(0, 1)
        chain(left, a12, down, 2)
        second(0, 0)
        chain(left, a12, down, 3)
        into[1] = dot(left[...], b12[...]).astype(jnp.bfloat16)
        send(1)
        second(0, 1)
        end(2)
        into[2] = dot(right[...], a21[...]).astype(jnp.bfloat16)
        send(2)
        mid[...] = dot(left[...], b11[...]).astype(jnp.bfloat16)
        end(0)
        into[0] = (a11[...] + dot(mid[...], a21[...])).astype(jnp.bfloat16)
        send(0)

    def parts(ref):
        return [ref.at[part] for part in range(4)]

    def layer_parts(layer):
        refl, tran, back = [layer_s.at[layer, kind] for kind in range(3)]
        return [refl, tran, tran, back]

    def nothing(*where):
        pass

    last = levels - 1
    assert lay == 2
    full_star(
        *layer_parts(0), *layer_parts(1), state.at[0],
        lambda part: send_far(0, 1, 0, part), nothing, nothing, nothing,
    )

    slot_end = sum(jnp.where(group >= (1 << k), 1, 0) for k in range(last))

    def one_level(level, distance):
        @pl.when(group >= distance)
        def _():
            full_star(
                *parts(land.at[level]), *parts(state.at[level]), state.at[level + 1],
                lambda part: send_far(level + 1, 2 * distance, level + 1, part),
                functools.partial(relay_first, level),
                functools.partial(relay_second, level),
                functools.partial(relay_end, level),
            )

        @pl.when(group < distance)
        def _():
            far_left(level)
            for part in (3, 1, 2, 0):
                send_far(level + 1, 2 * distance, slot_end, part)

        return 2 * distance

    lax.fori_loop(0, last, one_level, 1)

    half = 1 << last

    @pl.when(group < half)
    def _():
        out_ref[...] = state[slot_end, :, own]

    @pl.when(group >= half)
    def _():
        a11, a12, a21, a22 = parts(land.at[last])
        b11, b12, b21, b22 = parts(state.at[last])
        right_rows, left_rows = right.at[:rows], left.at[:rows]
        relay_first(last, 3, 0)
        relay_first(last, 3, 1)
        relay_second(last, 3, 0)
        relay_second(last, 3, 1)
        relay_end(last, 3)
        up[...] = dot(a22[...], b11[...]).astype(jnp.bfloat16)
        down[...] = dot(b11[...], a22[...]).astype(jnp.bfloat16)
        for half in range(HALVES):
            far_copy(last, 1, 0, 1, half).wait_recv()
        for repeat in range(REFL):
            chain(right_rows, b21.at[own], up, repeat)
            chain(left_rows, a12.at[own], down, repeat)
        relay_first(last, 2, 0)
        right_mid = dot(right_rows[...], a22[...]).astype(jnp.bfloat16)
        left_mid = dot(left_rows[...], b11[...]).astype(jnp.bfloat16)
        relay_first(last, 2, 1)
        out_ref[1] = dot(left_rows[...], b12[...]).astype(jnp.bfloat16)
        relay_second(last, 2, 0)
        out_ref[3] = (b22[own] + dot(right_mid, b12[...])).astype(jnp.bfloat16)
        relay_second(last, 2, 1)
        relay_end(last, 2)
        out_ref[2] = dot(right_rows[...], a21[...]).astype(jnp.bfloat16)
        for half in range(HALVES):
            far_copy(last, 1, 0, 0, half).wait_recv()
        out_ref[0] = (a11[own] + dot(left_mid, a21[...])).astype(jnp.bfloat16)

    for layer in range(lay):
        for_offsets(lambda offset: mode_copy(offset, layer).wait_send())
        share_copy(layer, 0, blk, cross).wait_send()
        share_copy(layer, 1, blk, sib).wait_send()
        share_copy(layer, 2, cross, sib).wait_send()
    for_offsets(lambda offset: aux_copy(offset).wait_send())
    for level in range(levels):
        reach = 1 << level
        sends = group + reach < n
        if level < last:
            sends = jnp.logical_and(sends, group >= reach)

        @pl.when(sends)
        def _(level=level):
            far_left(level)

        @pl.when(group >= reach)
        def _(level=level):
            for part in range(4) if level < last else (2, 3):
                for half in range(HALVES):
                    relay_copy(level, part, half, 0, blk, cross).wait_send()
                    relay_copy(level, part, half, 1, blk, sib).wait_send()
                    relay_copy(level, part, half, 2, cross, sib).wait_send()


def on_device(n, nb, mode_matrix, decay_rate, facet_refl):
    layers, mode_local = decay_rate.shape
    harm = n * mode_matrix.shape[1]
    lay = layers // n
    levels = n.bit_length() - 1
    refl = facet_refl.astype(jnp.float32)
    tran = jnp.sqrt(1.0 - refl * refl) * jnp.exp(-decay_rate.astype(jnp.float32))
    coeff = jnp.concatenate(
        [tran.reshape(n, lay, mode_local), refl.reshape(n, lay, mode_local)], axis=1
    )
    coeff = jnp.pad(coeff, ((0, 0), (0, 8 - 2 * lay), (0, 0)))
    copies = LANES // mode_local
    place = lax.broadcasted_iota(jnp.int32, (1, 1, LANES), 2) // mode_local
    aux = jnp.where(
        place == lax.rem(lax.axis_index("layer"), copies), jnp.tile(coeff, (1, 1, copies)), 0.0
    )
    square = (harm, harm)
    dma = pltpu.SemaphoreType.DMA
    vmem = pl.BlockSpec(memory_space=pltpu.VMEM)
    result = pl.pallas_call(
        functools.partial(stack_kernel, n, nb, levels),
        out_shape=jax.ShapeDtypeStruct((4, harm // nb, harm), jnp.bfloat16),
        in_specs=[vmem, vmem],
        out_specs=vmem,
        scratch_shapes=[
            pltpu.VMEM((nb, lay, n) + mode_matrix.shape[1:], jnp.bfloat16),
            pltpu.VMEM((n, 8, LANES), jnp.float32),
            pltpu.VMEM(square, jnp.bfloat16),
            pltpu.VMEM((2,) + square, jnp.bfloat16),
            pltpu.VMEM((lay, 3) + square, jnp.bfloat16),
            pltpu.VMEM((levels, 4) + square, jnp.bfloat16),
            pltpu.VMEM((levels, 4) + square, jnp.bfloat16),
        ]
        + [pltpu.VMEM(square, jnp.bfloat16)] * 5
        + [dma((n, lay))] * 2
        + [dma((n,))] * 2
        + [dma((lay, 3))] * 2
        + [dma((levels, 4, HALVES))] * 2
        + [dma((levels, 4, HALVES, 3))] * 2,
        compiler_params=pltpu.CompilerParams(
            collective_id=0, has_side_effects=True, vmem_limit_bytes=56 * 1024 * 1024
        ),
        cost_estimate=pl.CostEstimate(
            flops=2 * harm**3 * 60, bytes_accessed=2**20, transcendentals=0
        ),
    )(mode_matrix, aux)
    return result[None]


def solution(mesh):
    n, nb = mesh.shape["layer"], mesh.shape["blk"]
    placed = (P(None, "layer", "blk"), P(None, "layer"), P(None, "layer"))
    return jax.shard_map(
        functools.partial(on_device, n, nb),
        mesh=mesh,
        in_specs=placed,
        out_specs=P("layer", None, "blk", None),
        check_vma=False,
    )
```

time: 87 us -> 94.2 us (1.083)
  Pallas kernels: 83.4 us -> 90.6 us
    pallas_call x1, Pallas kernels: 83.4 us -> 90.6 us  [on_device(): pl.pallas_call(functools.partial(stack_kernel, n, nb, levels), out_shape=...]
where the time goes in v2:
time: 94.2 us; the launch traced here: 94 us
  Pallas kernels  90.6 us (96%)
  local copies, waits for them, and re-layouts  2.69 us (3%)
    pallas_call x1, Pallas kernels, on_device(): pl.pallas_call(functools.partial(stack_kernel, n, nb, levels), out_shape=...  90.6 us
    unnamed x5, local copies, waits for them, and re-layouts  2.56 us

profile of v2, /device:TPU:17, one launch (start us, length us, event | category | flops | bytes accessed | tf_op | source)
XLA Modules:
  0.0 94.0 jit_solution(8116181789564471617)
XLA Ops:
  0.0 0.0 copy-start.1
  0.0 0.0 copy-start
  0.0 0.7 copy-done.1
  0.7 0.0 copy-done
  0.8 0.1 tile.10
  0.9 0.6 broadcast_select_fusion.aux_ref
  1.5 90.6 %shard_map.37 = bf16[4,128,512]{2,1,0:T(8,128)(2,1)} custom-call(bf16[16,64,128]{2,1,0:T(8,128)(2,1)} %mode_ref.1, f32[8,8,128]{2,1,0:T(8,128)} %broadcast_select_fusion.aux_ref), custom_call_target="tpu_custom_call" | custom-call | flops 16106127360 | bytes 1048576 | tf_op jit(solution)/shard_map/pallas_call | solution.py:349
  92.1 1.9 %copy.5 = bf16[1,4,128,512]{3,2,1,0:T(8,128)(2,1)} copy(bf16[1,4,128,512]{3,2,1,0:T(8,128)(2,1)} %bitcast.4) | data formatting | bytes 1048576
  (5 shorter events, 0.1 us)
Async XLA Ops:
  0.0 0.7 copy-start.1
  0.0 0.7 copy-start

commit v3 on v2

--- a/solution.py
+++ b/solution.py
@@ -23,7 +23,7 @@
     mrecv, arecv, modes, scaled, layer_s, state, land,
     down, up, left, right, mid,
     mode_send, mode_recv, aux_send, aux_recv, share_send, share_recv,
-    far_send, far_recv, relay_send, relay_recv,
+    far_send, far_recv, relay_send, relay_recv, pair_send, pair_recv,
 ):
     group = lax.axis_index("layer")
     blk = lax.axis_index("blk")
@@ -35,10 +35,18 @@
     lay = mode_ref.shape[0] // n
     mode_local = harm // n
 
-    def block_rows(index):
-        return pl.ds(pl.multiple_of(index * rows, rows), rows)
-
-    own = block_rows(blk)
+    def place(quarter):
+        return lax.rem(quarter, 2) * (nb // 2) + lax.div(quarter, 2)
+
+    def fixed_place(quarter):
+        return quarter % 2 * (nb // 2) + quarter // 2
+
+    def cut(index):
+        return slice(index * rows, (index + 1) * rows)
+
+    own = pl.ds(pl.multiple_of(place(blk) * rows, rows), rows)
+    wing = harm // 2
+    half_rows = pl.ds(pl.multiple_of(lax.rem(blk, 2) * wing, wing), wing)
 
     barrier = pltpu.get_barrier_semaphore()
 
@@ -116,12 +124,14 @@
         share_copy(layer, 1, sib, sib).wait_recv()
         share_copy(layer, 2, sib_cross, sib).wait_recv()
         for piece in range(nb):
-            cols = slice(piece * rows, (piece + 1) * rows)
+            cols = cut(piece)
             wide = mrecv[piece, layer].astype(jnp.float32).reshape(harm, rows)
-            modes[:, cols] = wide.astype(jnp.bfloat16)
             coeff = windows[piece]
-            scaled[0, :, cols] = (wide * coeff[lay + layer][None]).astype(jnp.bfloat16)
-            scaled[1, :, cols] = (wide * coeff[layer][None]).astype(jnp.bfloat16)
+            for quarter in range(nb):
+                some, where = wide[cut(quarter)], cut(fixed_place(quarter))
+                modes[where, cols] = some.astype(jnp.bfloat16)
+                scaled[0, where, cols] = (some * coeff[lay + layer][None]).astype(jnp.bfloat16)
+                scaled[1, where, cols] = (some * coeff[layer][None]).astype(jnp.bfloat16)
         for kind in range(2):
             layer_s[layer, kind] = lax.dot_general(
                 modes[...], scaled[kind], (((1,), (1,)), ((), ())),
@@ -129,9 +139,9 @@
             ).astype(jnp.bfloat16)
         layer_s[layer, 2] = -layer_s[layer, 0]
 
-    def piece_rows(index, half):
+    def piece_rows(quarter, half):
         size = rows // HALVES
-        return pl.ds(pl.multiple_of(index * rows + half * size, size), size)
+        return pl.ds(pl.multiple_of(place(quarter) * rows + half * size, size), size)
 
     def far_copy(level, distance, slot, part, half):
         return pltpu.make_async_remote_copy(
@@ -154,6 +164,20 @@
             for half in range(HALVES):
                 far_copy(level, 1, 0, part, half).wait_send()
 
+    def pair_copy(slot, part, where):
+        return pltpu.make_async_remote_copy(
+            src_ref=state.at[slot, part, where],
+            dst_ref=state.at[slot, part, where],
+            send_sem=pair_send.at[slot, part],
+            recv_sem=pair_recv.at[slot, part],
+            device_id=(group, sib),
+            device_id_type=MESH,
+        )
+
+    def settle(slot):
+        for part in range(2):
+            pair_copy(slot, part, half_rows).wait_recv()
+
     def relay_copy(level, part, half, index, piece, other):
         where = land.at[level, part, piece_rows(piece, half)]
         return pltpu.make_async_remote_copy(
@@ -165,14 +189,18 @@
             device_id_type=MESH,
         )
 
-    def relay_first(level, part, half):
-        far_copy(level, 1, 0, part, half).wait_recv()
-        relay_copy(level, part, half, 0, blk, cross).start()
-        relay_copy(level, part, half, 1, blk, sib).start()
-
-    def relay_second(level, part, half):
-        relay_copy(level, part, half, 0, cross, cross).wait_recv()
-        relay_copy(level, part, half, 2, cross, sib).start()
+    def relay_first(level, part):
+        for half in range(HALVES):
+            far_copy(level, 1, 0, part, half).wait_recv()
+            relay_copy(level, part, half, 0, blk, cross).start()
+            if part >= 2:
+                relay_copy(level, part, half, 1, blk, sib).start()
+
+    def relay_second(level, part):
+        for half in range(HALVES):
+            relay_copy(level, part, half, 0, cross, cross).wait_recv()
+            if part >= 2:
+                relay_copy(level, part, half, 2, cross, sib).start()
 
     def relay_end(level, part):
         for half in range(HALVES):
@@ -183,47 +211,44 @@
         source = start if repeat == 0 else total
         total[...] = (start[...] + dot(source[...], coupling[...])).astype(jnp.bfloat16)
 
-    def full_star(a11, a12, a21, a22, b11, b12, b21, b22, into, send, first, second, end):
-        first(3, 0)
-        first(3, 1)
-        second(3, 0)
-        first(1, 0)
-        second(3, 1)
+    def full_star(upper, lower, slot, send, first, second, end, ready):
+        a11, a12, a21, a22 = upper
+        b11, b12, b21, b22 = lower
+        a11, a12, b21, b22 = [ref.at[half_rows] for ref in (a11, a12, b21, b22)]
+        into = [state.at[slot, part, half_rows] for part in range(4)]
+        first(3)
+        second(3)
+        ready()
         end(3)
         up[...] = dot(a22[...], b11[...]).astype(jnp.bfloat16)
-        first(1, 1)
+        first(2)
         chain(right, b21, up, 0)
-        second(1, 0)
         chain(right, b21, up, 1)
         chain(right, b21, up, 2)
-        second(1, 1)
+        second(2)
         chain(right, b21, up, 3)
         mid[...] = dot(right[...], a22[...]).astype(jnp.bfloat16)
-        into[3] = (b22[...] + dot(mid[...], b12[...])).astype(jnp.bfloat16)
+        into[3][...] = (b22[...] + dot(mid[...], b12[...])).astype(jnp.bfloat16)
         send(3)
-        first(2, 0)
+        end(2)
+        into[2][...] = dot(right[...], a21[...]).astype(jnp.bfloat16)
+        send(2)
         down[...] = dot(b11[...], a22[...]).astype(jnp.bfloat16)
-        first(2, 1)
-        end(1)
+        first(1)
+        second(1)
         chain(left, a12, down, 0)
-        second(2, 0)
-        first(0, 0)
         chain(left, a12, down, 1)
-        second(2, 1)
-        first(0, 1)
+        first(0)
         chain(left, a12, down, 2)
-        second(0, 0)
         chain(left, a12, down, 3)
-        into[1] = dot(left[...], b12[...]).astype(jnp.bfloat16)
+        into[1][...] = dot(left[...], b12[...]).astype(jnp.bfloat16)
         send(1)
-        second(0, 1)
-        end(2)
-        into[2] = dot(right[...], a21[...]).astype(jnp.bfloat16)
-        send(2)
+        pair_copy(slot, 1, half_rows).start()
         mid[...] = dot(left[...], b11[...]).astype(jnp.bfloat16)
-        end(0)
-        into[0] = (a11[...] + dot(mid[...], a21[...])).astype(jnp.bfloat16)
+        second(0)
+        into[0][...] = (a11[...] + dot(mid[...], a21[...])).astype(jnp.bfloat16)
         send(0)
+        pair_copy(slot, 0, half_rows).start()
 
     def parts(ref):
         return [ref.at[part] for part in range(4)]
@@ -236,71 +261,93 @@
         pass
 
     last = levels - 1
-    assert lay == 2
+    assert lay == 2 and nb == 4 and last >= 1
     full_star(
-        *layer_parts(0), *layer_parts(1), state.at[0],
-        lambda part: send_far(0, 1, 0, part), nothing, nothing, nothing,
+        layer_parts(0), layer_parts(1), 0,
+        lambda part: send_far(0, 1, 0, part), nothing, nothing, nothing, nothing,
     )
 
     slot_end = sum(jnp.where(group >= (1 << k), 1, 0) for k in range(last))
+    half = 1 << last
 
     def one_level(level, distance):
         @pl.when(group >= distance)
         def _():
             full_star(
-                *parts(land.at[level]), *parts(state.at[level]), state.at[level + 1],
+                parts(land.at[level]), parts(state.at[level]), level + 1,
                 lambda part: send_far(level + 1, 2 * distance, level + 1, part),
                 functools.partial(relay_first, level),
                 functools.partial(relay_second, level),
                 functools.partial(relay_end, level),
+                lambda: settle(level),
             )
 
         @pl.when(group < distance)
         def _():
             far_left(level)
-            for part in (3, 1, 2, 0):
+
+            @pl.when(jnp.logical_or(level == 0, 2 * group >= distance))
+            def _():
+                settle(level)
+
+            @pl.when(level == last - 2)
+            def _():
+                for part in (3, 2):
+                    send_far(last, half, slot_end, part)
+
+            for part in (3, 2):
+                @pl.when(jnp.logical_or(level < last - 1, 4 * group >= half))
+                def _(part=part):
+                    send_far(level + 1, 2 * distance, slot_end, part)
+            for part in (1, 0):
                 send_far(level + 1, 2 * distance, slot_end, part)
 
         return 2 * distance
 
     lax.fori_loop(0, last, one_level, 1)
-
-    half = 1 << last
 
     @pl.when(group < half)
     def _():
-        out_ref[...] = state[slot_end, :, own]
+        @pl.when(2 * group >= half)
+        def _():
+            settle(last)
+
+        for quarter in range(nb):
+            out_ref[:, :, cut(quarter)] = state[slot_end, :, own, cut(fixed_place(quarter))]
+
+    def put(part, value):
+        for quarter in range(nb):
+            out_ref[part, :, cut(quarter)] = value[:, cut(fixed_place(quarter))].astype(
+                jnp.bfloat16
+            )
 
     @pl.when(group >= half)
     def _():
         a11, a12, a21, a22 = parts(land.at[last])
         b11, b12, b21, b22 = parts(state.at[last])
         right_rows, left_rows = right.at[:rows], left.at[:rows]
-        relay_first(last, 3, 0)
-        relay_first(last, 3, 1)
-        relay_second(last, 3, 0)
-        relay_second(last, 3, 1)
+        relay_first(last, 3)
+        relay_first(last, 2)
+        relay_second(last, 3)
+        settle(last)
         relay_end(last, 3)
         up[...] = dot(a22[...], b11[...]).astype(jnp.bfloat16)
         down[...] = dot(b11[...], a22[...]).astype(jnp.bfloat16)
-        for half in range(HALVES):
-            far_copy(last, 1, 0, 1, half).wait_recv()
+        relay_second(last, 2)
+        for piece in range(HALVES):
+            far_copy(last, 1, 0, 1, piece).wait_recv()
         for repeat in range(REFL):
             chain(right_rows, b21.at[own], up, repeat)
             chain(left_rows, a12.at[own], down, repeat)
-        relay_first(last, 2, 0)
         right_mid = dot(right_rows[...], a22[...]).astype(jnp.bfloat16)
         left_mid = dot(left_rows[...], b11[...]).astype(jnp.bfloat16)
-        relay_first(last, 2, 1)
-        out_ref[1] = dot(left_rows[...], b12[...]).astype(jnp.bfloat16)
-        relay_second(last, 2, 0)
-        out_ref[3] = (b22[own] + dot(right_mid, b12[...])).astype(jnp.bfloat16)
-        relay_second(last, 2, 1)
+        put(1, dot(left_rows[...], b12[...]))
+        put(3, b22[own] + dot(right_mid, b12[...]))
         relay_end(last, 2)
-        out_ref[2] = dot(right_rows[...], a21[...]).astype(jnp.bfloat16)
-        for half in range(HALVES):
-            far_copy(last, 1, 0, 0, half).wait_recv()
-        out_ref[0] = (a11[own] + dot(left_mid, a21[...])).astype(jnp.bfloat16)
+        put(2, dot(right_rows[...], a21[...]))
+        for piece in range(HALVES):
+            far_copy(last, 1, 0, 0, piece).wait_recv()
+        put(0, a11[own] + dot(left_mid, a21[...]))
 
     for layer in range(lay):
         for_offsets(lambda offset: mode_copy(offset, layer).wait_send())
@@ -323,8 +370,14 @@
             for part in range(4) if level < last else (2, 3):
                 for half in range(HALVES):
                     relay_copy(level, part, half, 0, blk, cross).wait_send()
-                    relay_copy(level, part, half, 1, blk, sib).wait_send()
-                    relay_copy(level, part, half, 2, cross, sib).wait_send()
+                    if part >= 2:
+                        relay_copy(level, part, half, 1, blk, sib).wait_send()
+                        relay_copy(level, part, half, 2, cross, sib).wait_send()
+
+        @pl.when(2 * group >= reach if level else group >= 0)
+        def _(level=level):
+            for part in range(2):
+                pair_copy(level, part, half_rows).wait_send()
 
 
 def on_device(n, nb, mode_matrix, decay_rate, facet_refl):
@@ -360,12 +413,14 @@
             pltpu.VMEM((levels, 4) + square, jnp.bfloat16),
             pltpu.VMEM((levels, 4) + square, jnp.bfloat16),
         ]
-        + [pltpu.VMEM(square, jnp.bfloat16)] * 5
+        + [pltpu.VMEM(square, jnp.bfloat16)] * 2
+        + [pltpu.VMEM((harm // 2, harm), jnp.bfloat16)] * 3
         + [dma((n, lay))] * 2
         + [dma((n,))] * 2
         + [dma((lay, 3))] * 2
         + [dma((levels, 4, HALVES))] * 2
-        + [dma((levels, 4, HALVES, 3))] * 2,
+        + [dma((levels, 4, HALVES, 3))] * 2
+        + [dma((levels, 2))] * 2,
         compiler_params=pltpu.CompilerParams(
             collective_id=0, has_side_effects=True, vmem_limit_bytes=56 * 1024 * 1024
         ),

time: 94.2 us -> 84.2 us (0.89)
  the two profiles are of different devices: /device:TPU:17 before, /device:TPU:19 now
where the time goes in v3:
time: 84.2 us; the launch traced here: 84 us
  Pallas kernels  80.6 us (96%)
  local copies, waits for them, and re-layouts  2.69 us (3%)
    pallas_call x1, Pallas kernels, on_device(): pl.pallas_call(functools.partial(stack_kernel, n, nb, levels), out_shape=...  80.6 us
    unnamed x5, local copies, waits for them, and re-layouts  2.56 us

profile of v3, /device:TPU:19, one launch (start us, length us, event | category | flops | bytes accessed | tf_op | source)
XLA Modules:
  0.0 84.0 jit_solution(12986822555863724095)
XLA Ops:
  0.0 0.0 copy-start.1
  0.0 0.0 copy-start
  0.0 0.7 copy-done.1
  0.7 0.0 copy-done
  0.8 0.1 tile.10
  0.9 0.6 broadcast_select_fusion.aux_ref
  1.5 80.6 %shard_map.37 = bf16[4,128,512]{2,1,0:T(8,128)(2,1)} custom-call(bf16[16,64,128]{2,1,0:T(8,128)(2,1)} %mode_ref.1, f32[8,8,128]{2,1,0:T(8,128)} %broadcast_select_fusion.aux_ref), custom_call_target="tpu_custom_call" | custom-call | flops 16106127360 | bytes 1048576 | tf_op jit(solution)/shard_map/pallas_call | solution.py:402
  82.1 1.9 %copy.5 = bf16[1,4,128,512]{3,2,1,0:T(8,128)(2,1)} copy(bf16[1,4,128,512]{3,2,1,0:T(8,128)(2,1)} %bitcast.4) | data formatting | bytes 1048576
  (5 shorter events, 0.1 us)
Async XLA Ops:
  0.0 0.7 copy-start.1
  0.0 0.7 copy-start

commit v4 on v3

v4 whole, which is shorter than its diff:
```python
import functools

import jax
import jax.numpy as jnp
from jax import lax
from jax.experimental import pallas as pl
from jax.experimental.pallas import tpu as pltpu
from jax.sharding import PartitionSpec as P

REFL = 4
LANES = 128
HALVES = 2
MESH = pl.DeviceIdType.MESH


def dot(left_op, right_op):
    return jnp.dot(left_op, right_op, preferred_element_type=jnp.float32)


def stack_kernel(
    n, nb, levels,
    mode_ref, aux_ref, out_ref,
    mrecv, arecv, modes, scaled, layer_s, state, land,
    down, up, left, right, mid,
    mode_send, mode_recv, aux_send, aux_recv, share_send, share_recv,
    far_send, far_recv, relay_send, relay_recv, join_send, join_recv,
):
    group = lax.axis_index("layer")
    blk = lax.axis_index("blk")
    cross = lax.rem(blk + 2, nb)
    sib = blk + 1 - 2 * lax.rem(blk, 2)
    sib_cross = lax.rem(sib + 2, nb)
    harm = state.shape[-1]
    rows = harm // nb
    lay = mode_ref.shape[0] // n
    mode_local = harm // n

    def cut(index):
        return slice(index * rows, (index + 1) * rows)

    own = pl.ds(pl.multiple_of(blk * rows, rows), rows)

    barrier = pltpu.get_barrier_semaphore()

    def greet(offset, carry):
        pl.semaphore_signal(
            barrier, inc=1, device_id=(lax.rem(group + offset, n), blk), device_id_type=MESH
        )
        return carry

    lax.fori_loop(1, n, greet, 0)
    for other in (cross, sib):
        pl.semaphore_signal(barrier, inc=1, device_id=(group, other), device_id_type=MESH)
    pl.semaphore_wait(barrier, n + 1)

    def mode_copy(offset, layer):
        target = lax.rem(group + offset, n)
        return pltpu.make_async_remote_copy(
            src_ref=mode_ref.at[target * lay + layer],
            dst_ref=mrecv.at[blk, layer, group],
            send_sem=mode_send.at[offset, layer],
            recv_sem=mode_recv.at[offset, layer],
            device_id=(target, blk),
            device_id_type=MESH,
        )

    def aux_copy(offset):
        target = lax.rem(group + offset, n)
        return pltpu.make_async_remote_copy(
            src_ref=aux_ref.at[target],
            dst_ref=arecv.at[group],
            send_sem=aux_send.at[offset],
            recv_sem=aux_recv.at[offset],
            device_id=(target, blk),
            device_id_type=MESH,
        )

    def for_offsets(body):
        def step(offset, carry):
            body(offset)
            return carry

        lax.fori_loop(1, n, step, 0)

    for layer in range(lay):
        for_offsets(lambda offset: mode_copy(offset, layer).start())
        if layer == 0:
            for_offsets(lambda offset: aux_copy(offset).start())
        mrecv[blk, layer, group] = mode_ref[group * lay + layer]
    arecv[group] = aux_ref[group]

    def share_copy(layer, offset, index, piece, other):
        where = mrecv.at[piece, layer, lax.rem(group + n - offset, n)]
        return pltpu.make_async_remote_copy(
            src_ref=where,
            dst_ref=where,
            send_sem=share_send.at[layer, offset, index],
            recv_sem=share_recv.at[layer, offset, index],
            device_id=(group, other),
            device_id_type=MESH,
        )

    def share_first(layer, offset):
        share_copy(layer, offset, 0, blk, cross).start()
        share_copy(layer, offset, 1, blk, sib).start()

    def share_second(layer):
        def step(offset, carry):
            share_copy(layer, offset, 0, cross, cross).wait_recv()
            share_copy(layer, offset, 2, cross, sib).start()
            return carry

        lax.fori_loop(0, n, step, 0)

    def share_end(layer):
        def step(offset, carry):
            share_copy(layer, offset, 1, sib, sib).wait_recv()
            share_copy(layer, offset, 2, sib_cross, sib).wait_recv()
            return carry

        lax.fori_loop(0, n, step, 0)

    def share_left(layer):
        def step(offset, carry):
            share_copy(layer, offset, 0, blk, cross).wait_send()
            share_copy(layer, offset, 1, blk, sib).wait_send()
            share_copy(layer, offset, 2, cross, sib).wait_send()
            return carry

        lax.fori_loop(0, n, step, 0)

    for layer in range(lay):
        share_first(layer, 0)
    for layer in range(lay):
        def pass_on(offset, layer=layer):
            mode_copy(offset, layer).wait_recv()
            share_first(layer, offset)

        for_offsets(pass_on)
    for_offsets(lambda offset: aux_copy(offset).wait_recv())
    per_window = LANES // mode_local
    windows = [
        sum(arecv[index] for index in range(w * per_window, (w + 1) * per_window))
        for w in range(harm // LANES)
    ]

    share_second(0)
    for layer in range(lay):
        share_end(layer)
        if layer + 1 < lay:
            share_second(layer + 1)
        for piece in range(nb):
            cols = cut(piece)
            wide = mrecv[piece, layer].astype(jnp.float32).reshape(harm, rows)
            coeff = windows[piece]
            modes[:, cols] = wide.astype(jnp.bfloat16)
            scaled[0, :, cols] = (wide * coeff[lay + layer][None]).astype(jnp.bfloat16)
            scaled[1, :, cols] = (wide * coeff[layer][None]).astype(jnp.bfloat16)
        for kind in range(2):
            layer_s[layer, kind] = lax.dot_general(
                modes[...], scaled[kind], (((1,), (1,)), ((), ())),
                preferred_element_type=jnp.float32,
            ).astype(jnp.bfloat16)
        layer_s[layer, 2] = -layer_s[layer, 0]

    def piece_rows(quarter, half):
        size = rows // HALVES
        return pl.ds(pl.multiple_of(quarter * rows + half * size, size), size)

    def far_copy(level, distance, slot, part, half):
        return pltpu.make_async_remote_copy(
            src_ref=state.at[slot, part, piece_rows(blk, half)],
            dst_ref=land.at[level, part, piece_rows(blk, half)],
            send_sem=far_send.at[level, part, half],
            recv_sem=far_recv.at[level, part, half],
            device_id=(lax.rem(group + distance, n), blk),
            device_id_type=MESH,
        )

    def send_far(level, distance, slot, part):
        @pl.when(group + distance < n)
        def _():
            for half in range(HALVES):
                far_copy(level, distance, slot, part, half).start()

    def far_left(level):
        for part in range(4):
            for half in range(HALVES):
                far_copy(level, 1, 0, part, half).wait_send()

    def join_copy(slot, part, index, quarter, other):
        where = state.at[slot, part, pl.ds(pl.multiple_of(quarter * rows, rows), rows)]
        return pltpu.make_async_remote_copy(
            src_ref=where,
            dst_ref=where,
            send_sem=join_send.at[slot, part, index],
            recv_sem=join_recv.at[slot, part, index],
            device_id=(group, other),
            device_id_type=MESH,
        )

    def join_first(slot, part):
        join_copy(slot, part, 0, blk, cross).start()
        join_copy(slot, part, 1, blk, sib).start()

    def join_second(slot):
        for part in (1, 0):
            join_copy(slot, part, 0, cross, cross).wait_recv()
            join_copy(slot, part, 2, cross, sib).start()

    def join_end(slot):
        for part in (1, 0):
            join_copy(slot, part, 1, sib, sib).wait_recv()
            join_copy(slot, part, 2, sib_cross, sib).wait_recv()

    def relay_copy(level, part, half, index, piece, other):
        where = land.at[level, part, piece_rows(piece, half)]
        return pltpu.make_async_remote_copy(
            src_ref=where,
            dst_ref=where,
            send_sem=relay_send.at[level, part, half, index],
            recv_sem=relay_recv.at[level, part, half, index],
            device_id=(group, other),
            device_id_type=MESH,
        )

    def relay_first(level, part):
        for half in range(HALVES):
            far_copy(level, 1, 0, part, half).wait_recv()
            if part >= 2:
                relay_copy(level, part, half, 0, blk, cross).start()
                relay_copy(level, part, half, 1, blk, sib).start()

    def relay_second(level, part):
        for half in range(HALVES):
            relay_copy(level, part, half, 0, cross, cross).wait_recv()
            relay_copy(level, part, half, 2, cross, sib).start()

    def relay_end(level, part):
        for half in range(HALVES):
            relay_copy(level, part, half, 1, sib, sib).wait_recv()
            relay_copy(level, part, half, 2, sib_cross, sib).wait_recv()

    def chain(total, start, coupling, repeat):
        source = start if repeat == 0 else total
        total[...] = (start[...] + dot(source[...], coupling[...])).astype(jnp.bfloat16)

    def own_star(upper, lower, put, first, second, end, join):
        a11, a12, a21, a22 = upper
        b11, b12, b21, b22 = lower
        a11, a12, b21, b22 = [ref.at[own] for ref in (a11, a12, b21, b22)]
        first(3)
        join(0)
        second(3)
        join(1)
        end(3)
        up[...] = dot(a22[...], b11[...]).astype(jnp.bfloat16)
        for repeat in range(REFL):
            chain(right, b21, up, repeat)
        mid[...] = dot(right[...], a22[...]).astype(jnp.bfloat16)
        put(3, b22[...] + dot(mid[...], b12[...]))
        down[...] = dot(b11[...], a22[...]).astype(jnp.bfloat16)
        first(1)
        first(2)
        for repeat in range(REFL):
            chain(left, a12, down, repeat)
        put(1, dot(left[...], b12[...]))
        mid[...] = dot(left[...], b11[...]).astype(jnp.bfloat16)
        second(2)
        end(2)
        put(2, dot(right[...], a21[...]))
        first(0)
        put(0, a11[...] + dot(mid[...], a21[...]))

    def parts(ref):
        return [ref.at[part] for part in range(4)]

    def layer_parts(layer):
        refl, tran, back = [layer_s.at[layer, kind] for kind in range(3)]
        return [refl, tran, tran, back]

    def nothing(*where):
        pass

    last = levels - 1
    assert lay == 2 and nb == 4 and last >= 1
    def put_state(level, distance):
        def put(part, value):
            state[level, part, own] = value.astype(jnp.bfloat16)
            send_far(level, distance, level, part)
            if part < 2:
                join_first(level, part)

        return put

    own_star(
        layer_parts(0), layer_parts(1), put_state(0, 1), nothing, nothing, nothing, nothing
    )

    slot_end = sum(jnp.where(group >= (1 << k), 1, 0) for k in range(last))
    half = 1 << last

    def one_level(level, distance):
        @pl.when(group >= distance)
        def _():
            own_star(
                parts(land.at[level]), parts(state.at[level]), put_state(level + 1, 2 * distance),
                functools.partial(relay_first, level),
                functools.partial(relay_second, level),
                functools.partial(relay_end, level),
                lambda step: (join_second, join_end)[step](level),
            )

        @pl.when(group < distance)
        def _():
            @pl.when(jnp.logical_or(level == 0, 2 * group >= distance))
            def _():
                join_second(level)
                join_end(level)

            far_left(level)

            @pl.when(level == last - 2)
            def _():
                for part in (3, 1):
                    send_far(last, half, slot_end, part)

            for part in (3, 1):
                @pl.when(jnp.logical_or(level < last - 1, 4 * group >= half))
                def _(part=part):
                    send_far(level + 1, 2 * distance, slot_end, part)
            for part in (2, 0):
                send_far(level + 1, 2 * distance, slot_end, part)

        return 2 * distance

    lax.fori_loop(0, last, one_level, 1)

    @pl.when(group < half)
    def _():
        @pl.when(2 * group >= half)
        def _():
            join_second(last)
            join_end(last)

        out_ref[...] = state[slot_end, :, own]

    def put_out(part, value):
        out_ref[part] = value.astype(jnp.bfloat16)

    @pl.when(group >= half)
    def _():
        own_star(
            parts(land.at[last]), parts(state.at[last]), put_out,
            functools.partial(relay_first, last),
            functools.partial(relay_second, last),
            functools.partial(relay_end, last),
            lambda step: (join_second, join_end)[step](last),
        )

    for layer in range(lay):
        for_offsets(lambda offset: mode_copy(offset, layer).wait_send())
        share_left(layer)
    for_offsets(lambda offset: aux_copy(offset).wait_send())
    for level in range(levels):
        reach = 1 << level
        sends = group + reach < n
        if level < last:
            sends = jnp.logical_and(sends, group >= reach)

        @pl.when(sends)
        def _(level=level):
            far_left(level)

        @pl.when(group >= reach)
        def _(level=level):
            for part in (2, 3):
                for piece in range(HALVES):
                    relay_copy(level, part, piece, 0, blk, cross).wait_send()
                    relay_copy(level, part, piece, 1, blk, sib).wait_send()
                    relay_copy(level, part, piece, 2, cross, sib).wait_send()

        @pl.when(2 * group >= reach if level else group >= 0)
        def _(level=level):
            for part in range(2):
                join_copy(level, part, 0, blk, cross).wait_send()
                join_copy(level, part, 1, blk, sib).wait_send()
                join_copy(level, part, 2, cross, sib).wait_send()


def on_device(n, nb, mode_matrix, decay_rate, facet_refl):
    layers, mode_local = decay_rate.shape
    harm = n * mode_matrix.shape[1]
    lay = layers // n
    levels = n.bit_length() - 1
    refl = facet_refl.astype(jnp.float32)
    tran = jnp.sqrt(1.0 - refl * refl) * jnp.exp(-decay_rate.astype(jnp.float32))
    coeff = jnp.concatenate(
        [tran.reshape(n, lay, mode_local), refl.reshape(n, lay, mode_local)], axis=1
    )
    coeff = jnp.pad(coeff, ((0, 0), (0, 8 - 2 * lay), (0, 0)))
    copies = LANES // mode_local
    place = lax.broadcasted_iota(jnp.int32, (1, 1, LANES), 2) // mode_local
    aux = jnp.where(
        place == lax.rem(lax.axis_index("layer"), copies), jnp.tile(coeff, (1, 1, copies)), 0.0
    )
    square = (harm, harm)
    dma = pltpu.SemaphoreType.DMA
    vmem = pl.BlockSpec(memory_space=pltpu.VMEM)
    result = pl.pallas_call(
        functools.partial(stack_kernel, n, nb, levels),
        out_shape=jax.ShapeDtypeStruct((4, harm // nb, harm), jnp.bfloat16),
        in_specs=[vmem, vmem],
        out_specs=vmem,
        scratch_shapes=[
            pltpu.VMEM((nb, lay, n) + mode_matrix.shape[1:], jnp.bfloat16),
            pltpu.VMEM((n, 8, LANES), jnp.float32),
            pltpu.VMEM(square, jnp.bfloat16),
            pltpu.VMEM((2,) + square, jnp.bfloat16),
            pltpu.VMEM((lay, 3) + square, jnp.bfloat16),
            pltpu.VMEM((levels, 4) + square, jnp.bfloat16),
            pltpu.VMEM((levels, 4) + square, jnp.bfloat16),
        ]
        + [pltpu.VMEM(square, jnp.bfloat16)] * 2
        + [pltpu.VMEM((harm // nb, harm), jnp.bfloat16)] * 3
        + [dma((n, lay))] * 2
        + [dma((n,))] * 2
        + [dma((lay, n, 3))] * 2
        + [dma((levels, 4, HALVES))] * 2
        + [dma((levels, 4, HALVES, 3))] * 2
        + [dma((levels, 2, 3))] * 2,
        compiler_params=pltpu.CompilerParams(
            collective_id=0, has_side_effects=True, vmem_limit_bytes=56 * 1024 * 1024
        ),
        cost_estimate=pl.CostEstimate(
            flops=2 * harm**3 * 60, bytes_accessed=2**20, transcendentals=0
        ),
    )(mode_matrix, aux)
    return result[None]


def solution(mesh):
    n, nb = mesh.shape["layer"], mesh.shape["blk"]
    placed = (P(None, "layer", "blk"), P(None, "layer"), P(None, "layer"))
    return jax.shard_map(
        functools.partial(on_device, n, nb),
        mesh=mesh,
        in_specs=placed,
        out_specs=P("layer", None, "blk", None),
        check_vma=False,
    )
```

time: 84.2 us -> 82 us (0.974)
  the two profiles are of different devices: /device:TPU:19 before, /device:TPU:28 now
where the time goes in v4:
time: 82 us; the launch traced here: 80.9 us
  Pallas kernels  77.5 us (95%)
  local copies, waits for them, and re-layouts  2.69 us (3%)
    pallas_call x1, Pallas kernels, on_device(): pl.pallas_call(functools.partial(stack_kernel, n, nb, levels), out_shape=...  77.5 us
    unnamed x5, local copies, waits for them, and re-layouts  2.56 us

profile of v4, /device:TPU:28, one launch (start us, length us, event | category | flops | bytes accessed | tf_op | source)
XLA Modules:
  0.0 80.9 jit_solution(6774715658155559613)
XLA Ops:
  0.0 0.0 copy-start.1
  0.0 0.0 copy-start
  0.0 0.7 copy-done.1
  0.7 0.0 copy-done
  0.8 0.1 tile.10
  0.9 0.6 broadcast_select_fusion.aux_ref
  1.5 77.5 %shard_map.37 = bf16[4,128,512]{2,1,0:T(8,128)(2,1)} custom-call(bf16[16,64,128]{2,1,0:T(8,128)(2,1)} %mode_ref.1, f32[8,8,128]{2,1,0:T(8,128)} %broadcast_select_fusion.aux_ref), custom_call_target="tpu_custom_call" | custom-call | flops 16106127360 | bytes 1048576 | tf_op jit(solution)/shard_map/pallas_call | solution.py:410
  79.0 1.9 %copy.5 = bf16[1,4,128,512]{3,2,1,0:T(8,128)(2,1)} copy(bf16[1,4,128,512]{3,2,1,0:T(8,128)(2,1)} %bitcast.4) | data formatting | bytes 1048576
  (5 shorter events, 0.1 us)
Async XLA Ops:
  0.0 0.7 copy-start.1
  0.0 0.7 copy-start

commit v5 on v4

--- a/solution.py
+++ b/solution.py
@@ -33,6 +33,10 @@
     harm = state.shape[-1]
     rows = harm // nb
     lay = mode_ref.shape[0] // n
+    last = levels - 1
+    half = 1 << last
+    quarter = half // 2
+    middle = jnp.logical_and(group >= half, group < half + quarter)
     mode_local = harm // n
 
     def cut(index):
@@ -177,11 +181,15 @@
             device_id_type=MESH,
         )
 
+    def start_far(level, distance, slot, part):
+        for half in range(HALVES):
+            far_copy(level, distance, slot, part, half).start()
+
     def send_far(level, distance, slot, part):
-        @pl.when(group + distance < n)
-        def _():
-            for half in range(HALVES):
-                far_copy(level, distance, slot, part, half).start()
+        sends = jnp.logical_and(
+            group + distance < n, jnp.logical_or(level != last, group < quarter)
+        )
+        pl.when(sends)(lambda: start_far(level, distance, slot, part))
 
     def far_left(level):
         for part in range(4):
@@ -224,12 +232,18 @@
             device_id_type=MESH,
         )
 
-    def relay_first(level, part):
+    def relay_first(level, part, near=None):
         for half in range(HALVES):
             far_copy(level, 1, 0, part, half).wait_recv()
-            if part >= 2:
+
+            def pass_on(half=half):
                 relay_copy(level, part, half, 0, blk, cross).start()
                 relay_copy(level, part, half, 1, blk, sib).start()
+
+            if part >= 2:
+                pass_on()
+            elif near is not None:
+                pl.when(near)(pass_on)
 
     def relay_second(level, part):
         for half in range(HALVES):
@@ -282,8 +296,7 @@
     def nothing(*where):
         pass
 
-    last = levels - 1
-    assert lay == 2 and nb == 4 and last >= 1
+    assert lay == 2 and nb == 4 and last >= 2
     def put_state(level, distance):
         def put(part, value):
             state[level, part, own] = value.astype(jnp.bfloat16)
@@ -298,14 +311,15 @@
     )
 
     slot_end = sum(jnp.where(group >= (1 << k), 1, 0) for k in range(last))
-    half = 1 << last
 
     def one_level(level, distance):
         @pl.when(group >= distance)
         def _():
             own_star(
                 parts(land.at[level]), parts(state.at[level]), put_state(level + 1, 2 * distance),
-                functools.partial(relay_first, level),
+                functools.partial(
+                    relay_first, level, near=jnp.logical_and(level == last - 1, middle)
+                ),
                 functools.partial(relay_second, level),
                 functools.partial(relay_end, level),
                 lambda step: (join_second, join_end)[step](level),
@@ -336,6 +350,27 @@
 
     lax.fori_loop(0, last, one_level, 1)
 
+    @pl.when(middle)
+    def _():
+        def near_join(step):
+            for part in (1, 0):
+                (relay_second, relay_end)[step](last - 1, part)
+
+        def put_on(part, value):
+            state[levels, part, own] = value.astype(jnp.bfloat16)
+            start_far(last, quarter, levels, part)
+
+        own_star(
+            parts(land.at[last]), parts(land.at[last - 1]), put_on,
+            functools.partial(relay_first, last),
+            functools.partial(relay_second, last),
+            functools.partial(relay_end, last),
+            near_join,
+        )
+
+    def unless_middle(act):
+        return lambda part: pl.when(jnp.logical_not(middle))(lambda: act(last, part))
+
     @pl.when(group < half)
     def _():
         @pl.when(2 * group >= half)
@@ -352,9 +387,9 @@
     def _():
         own_star(
             parts(land.at[last]), parts(state.at[last]), put_out,
-            functools.partial(relay_first, last),
-            functools.partial(relay_second, last),
-            functools.partial(relay_end, last),
+            unless_middle(relay_first),
+            unless_middle(relay_second),
+            unless_middle(relay_end),
             lambda step: (join_second, join_end)[step](last),
         )
 
@@ -367,6 +402,8 @@
         sends = group + reach < n
         if level < last:
             sends = jnp.logical_and(sends, group >= reach)
+        else:
+            sends = jnp.logical_or(group < quarter, middle)
 
         @pl.when(sends)
         def _(level=level):
@@ -379,6 +416,15 @@
                     relay_copy(level, part, piece, 0, blk, cross).wait_send()
                     relay_copy(level, part, piece, 1, blk, sib).wait_send()
                     relay_copy(level, part, piece, 2, cross, sib).wait_send()
+
+        if level == last - 1:
+            @pl.when(middle)
+            def _(level=level):
+                for part in range(2):
+                    for piece in range(HALVES):
+                        relay_copy(level, part, piece, 0, blk, cross).wait_send()
+                        relay_copy(level, part, piece, 1, blk, sib).wait_send()
+                        relay_copy(level, part, piece, 2, cross, sib).wait_send()
 
         @pl.when(2 * group >= reach if level else group >= 0)
         def _(level=level):
@@ -418,7 +464,7 @@
             pltpu.VMEM(square, jnp.bfloat16),
             pltpu.VMEM((2,) + square, jnp.bfloat16),
             pltpu.VMEM((lay, 3) + square, jnp.bfloat16),
-            pltpu.VMEM((levels, 4) + square, jnp.bfloat16),
+            pltpu.VMEM((levels + 1, 4) + square, jnp.bfloat16),
             pltpu.VMEM((levels, 4) + square, jnp.bfloat16),
         ]
         + [pltpu.VMEM(square, jnp.bfloat16)] * 2

time: 82 us -> 96.9 us (1.18)
  Pallas kernels: 77.5 us -> 92.4 us
    pallas_call x1, Pallas kernels: 77.5 us -> 92.4 us  [on_device(): pl.pallas_call(functools.partial(stack_kernel, n, nb, levels), out_shape=...]
where the time goes in v5:
time: 96.9 us; the launch traced here: 95.8 us
  Pallas kernels  92.4 us (95%)
  local copies, waits for them, and re-layouts  2.69 us (3%)
    pallas_call x1, Pallas kernels, on_device(): pl.pallas_call(functools.partial(stack_kernel, n, nb, levels), out_shape=...  92.4 us
    unnamed x5, local copies, waits for them, and re-layouts  2.56 us

profile of v5, /device:TPU:28, one launch (start us, length us, event | category | flops | bytes accessed | tf_op | source)
XLA Modules:
  0.0 95.8 jit_solution(11759464317835389331)
XLA Ops:
  0.0 0.0 copy-start.1
  0.0 0.0 copy-start
  0.0 0.7 copy-done.1
  0.7 0.0 copy-done
  0.8 0.1 tile.10
  0.9 0.6 broadcast_select_fusion.aux_ref
  1.5 92.4 %shard_map.37 = bf16[4,128,512]{2,1,0:T(8,128)(2,1)} custom-call(bf16[16,64,128]{2,1,0:T(8,128)(2,1)} %mode_ref.1, f32[8,8,128]{2,1,0:T(8,128)} %broadcast_select_fusion.aux_ref), custom_call_target="tpu_custom_call" | custom-call | flops 16106127360 | bytes 1048576 | tf_op jit(solution)/shard_map/pallas_call | solution.py:456
  93.9 1.9 %copy.5 = bf16[1,4,128,512]{3,2,1,0:T(8,128)(2,1)} copy(bf16[1,4,128,512]{3,2,1,0:T(8,128)(2,1)} %bitcast.4) | data formatting | bytes 1048576
  (5 shorter events, 0.1 us)
Async XLA Ops:
  0.0 0.7 copy-start.1
  0.0 0.7 copy-start

commit v6 on v4

--- a/solution.py
+++ b/solution.py
@@ -21,9 +21,10 @@
     n, nb, levels,
     mode_ref, aux_ref, out_ref,
     mrecv, arecv, modes, scaled, layer_s, state, land,
-    down, up, left, right, mid,
+    up, total, mid,
     mode_send, mode_recv, aux_send, aux_recv, share_send, share_recv,
     far_send, far_recv, relay_send, relay_recv, join_send, join_recv,
+    swap_send, swap_recv,
 ):
     group = lax.axis_index("layer")
     blk = lax.axis_index("blk")
@@ -38,7 +39,16 @@
     def cut(index):
         return slice(index * rows, (index + 1) * rows)
 
+    role = lax.rem(blk, 2)
+    lead_part, next_part = 3 - 2 * role, 2 - 2 * role
     own = pl.ds(pl.multiple_of(blk * rows, rows), rows)
+    sib_own = pl.ds(pl.multiple_of(sib * rows, rows), rows)
+    wing = 2 * rows
+
+    def wing_of(device):
+        return pl.ds(pl.multiple_of(lax.div(device, 2) * wing, wing), wing)
+
+    mine = wing_of(blk)
 
     barrier = pltpu.get_barrier_semaphore()
 
@@ -163,9 +173,9 @@
             ).astype(jnp.bfloat16)
         layer_s[layer, 2] = -layer_s[layer, 0]
 
-    def piece_rows(quarter, half):
-        size = rows // HALVES
-        return pl.ds(pl.multiple_of(quarter * rows + half * size, size), size)
+    def piece_rows(device, half):
+        size = wing // HALVES
+        return pl.ds(pl.multiple_of(lax.div(device, 2) * wing + half * size, size), size)
 
     def far_copy(level, distance, slot, part, half):
         return pltpu.make_async_remote_copy(
@@ -184,12 +194,16 @@
                 far_copy(level, distance, slot, part, half).start()
 
     def far_left(level):
-        for part in range(4):
+        for part in (lead_part, next_part):
             for half in range(HALVES):
                 far_copy(level, 1, 0, part, half).wait_send()
 
-    def join_copy(slot, part, index, quarter, other):
-        where = state.at[slot, part, pl.ds(pl.multiple_of(quarter * rows, rows), rows)]
+    def far_end(level, part):
+        for half in range(HALVES):
+            far_copy(level, 1, 0, part, half).wait_recv()
+
+    def join_copy(slot, part, index, device, other):
+        where = state.at[slot, part, wing_of(device)]
         return pltpu.make_async_remote_copy(
             src_ref=where,
             dst_ref=where,
@@ -213,8 +227,12 @@
             join_copy(slot, part, 1, sib, sib).wait_recv()
             join_copy(slot, part, 2, sib_cross, sib).wait_recv()
 
-    def relay_copy(level, part, half, index, piece, other):
-        where = land.at[level, part, piece_rows(piece, half)]
+    def join(slot):
+        pl.when(role == 1)(lambda: join_second(slot))
+        pl.when(role == 0)(lambda: join_end(slot))
+
+    def relay_copy(level, part, half, index, device, other):
+        where = land.at[level, part, piece_rows(device, half)]
         return pltpu.make_async_remote_copy(
             src_ref=where,
             dst_ref=where,
@@ -227,9 +245,8 @@
     def relay_first(level, part):
         for half in range(HALVES):
             far_copy(level, 1, 0, part, half).wait_recv()
-            if part >= 2:
-                relay_copy(level, part, half, 0, blk, cross).start()
-                relay_copy(level, part, half, 1, blk, sib).start()
+            relay_copy(level, part, half, 0, blk, cross).start()
+            relay_copy(level, part, half, 1, blk, sib).start()
 
     def relay_second(level, part):
         for half in range(HALVES):
@@ -241,36 +258,67 @@
             relay_copy(level, part, half, 1, sib, sib).wait_recv()
             relay_copy(level, part, half, 2, sib_cross, sib).wait_recv()
 
+    def swap_copy(slot, part):
+        return pltpu.make_async_remote_copy(
+            src_ref=state.at[slot, part, sib_own],
+            dst_ref=out_ref.at[part],
+            send_sem=swap_send.at[part],
+            recv_sem=swap_recv.at[part],
+            device_id=(group, sib),
+            device_id_type=MESH,
+        )
+
+    def put_out(slot, part):
+        swap_copy(slot, part).start()
+        out_ref[part] = state[slot, part, own]
+
     def chain(total, start, coupling, repeat):
         source = start if repeat == 0 else total
         total[...] = (start[...] + dot(source[...], coupling[...])).astype(jnp.bfloat16)
 
-    def own_star(upper, lower, put, first, second, end, join):
+    def under_star(upper, lower, put, level):
         a11, a12, a21, a22 = upper
         b11, b12, b21, b22 = lower
-        a11, a12, b21, b22 = [ref.at[own] for ref in (a11, a12, b21, b22)]
-        first(3)
-        join(0)
-        second(3)
-        join(1)
-        end(3)
+        b21, b22 = b21.at[mine], b22.at[mine]
+        if level is not None:
+            relay_first(level, 3)
+            join_end(level)
+            relay_second(level, 3)
         up[...] = dot(a22[...], b11[...]).astype(jnp.bfloat16)
+        chain(total, b21, up, 0)
+        chain(total, b21, up, 1)
+        if level is not None:
+            relay_first(level, 2)
+        chain(total, b21, up, 2)
+        chain(total, b21, up, 3)
+        mid[...] = dot(total[...], a22[...]).astype(jnp.bfloat16)
+        put(3, b22[...] + dot(mid[...], b12[...]))
+        if level is not None:
+            relay_second(level, 2)
+        put(2, dot(total[...], a21[...]))
+
+    def over_star(upper, lower, put, level):
+        a11, a12, a21, a22 = upper
+        b11, b12, b21, b22 = lower
+        a11, a12 = a11.at[mine], a12.at[mine]
+        if level is not None:
+            join_second(level)
+            relay_end(level, 3)
+        up[...] = dot(b11[...], a22[...]).astype(jnp.bfloat16)
+        if level is not None:
+            far_end(level, 1)
         for repeat in range(REFL):
-            chain(right, b21, up, repeat)
-        mid[...] = dot(right[...], a22[...]).astype(jnp.bfloat16)
-        put(3, b22[...] + dot(mid[...], b12[...]))
-        down[...] = dot(b11[...], a22[...]).astype(jnp.bfloat16)
-        first(1)
-        first(2)
-        for repeat in range(REFL):
-            chain(left, a12, down, repeat)
-        put(1, dot(left[...], b12[...]))
-        mid[...] = dot(left[...], b11[...]).astype(jnp.bfloat16)
-        second(2)
-        end(2)
-        put(2, dot(right[...], a21[...]))
-        first(0)
+            chain(total, a12, up, repeat)
+        put(1, dot(total[...], b12[...]))
+        mid[...] = dot(total[...], b11[...]).astype(jnp.bfloat16)
+        if level is not None:
+            far_end(level, 0)
+            relay_end(level, 2)
         put(0, a11[...] + dot(mid[...], a21[...]))
+
+    def star(upper, lower, put, level):
+        pl.when(role == 0)(lambda: under_star(upper, lower, put, level))
+        pl.when(role == 1)(lambda: over_star(upper, lower, put, level))
 
     def parts(ref):
         return [ref.at[part] for part in range(4)]
@@ -279,23 +327,19 @@
         refl, tran, back = [layer_s.at[layer, kind] for kind in range(3)]
         return [refl, tran, tran, back]
 
-    def nothing(*where):
-        pass
-
     last = levels - 1
     assert lay == 2 and nb == 4 and last >= 1
+
     def put_state(level, distance):
         def put(part, value):
-            state[level, part, own] = value.astype(jnp.bfloat16)
+            state[level, part, mine] = value.astype(jnp.bfloat16)
             send_far(level, distance, level, part)
             if part < 2:
                 join_first(level, part)
 
         return put
 
-    own_star(
-        layer_parts(0), layer_parts(1), put_state(0, 1), nothing, nothing, nothing, nothing
-    )
+    star(layer_parts(0), layer_parts(1), put_state(0, 1), None)
 
     slot_end = sum(jnp.where(group >= (1 << k), 1, 0) for k in range(last))
     half = 1 << last
@@ -303,34 +347,28 @@
     def one_level(level, distance):
         @pl.when(group >= distance)
         def _():
-            own_star(
-                parts(land.at[level]), parts(state.at[level]), put_state(level + 1, 2 * distance),
-                functools.partial(relay_first, level),
-                functools.partial(relay_second, level),
-                functools.partial(relay_end, level),
-                lambda step: (join_second, join_end)[step](level),
+            star(
+                parts(land.at[level]), parts(state.at[level]),
+                put_state(level + 1, 2 * distance), level,
             )
 
         @pl.when(group < distance)
         def _():
             @pl.when(jnp.logical_or(level == 0, 2 * group >= distance))
             def _():
-                join_second(level)
-                join_end(level)
+                join(level)
 
             far_left(level)
 
             @pl.when(level == last - 2)
             def _():
-                for part in (3, 1):
-                    send_far(last, half, slot_end, part)
-
-            for part in (3, 1):
-                @pl.when(jnp.logical_or(level < last - 1, 4 * group >= half))
-                def _(part=part):
-                    send_far(level + 1, 2 * distance, slot_end, part)
-            for part in (2, 0):
-                send_far(level + 1, 2 * distance, slot_end, part)
+                send_far(last, half, slot_end, lead_part)
+
+            @pl.when(jnp.logical_or(level < last - 1, 4 * group >= half))
+            def _():
+                send_far(level + 1, 2 * distance, slot_end, lead_part)
+
+            send_far(level + 1, 2 * distance, slot_end, next_part)
 
         return 2 * distance
 
@@ -340,23 +378,21 @@
     def _():
         @pl.when(2 * group >= half)
         def _():
-            join_second(last)
-            join_end(last)
-
-        out_ref[...] = state[slot_end, :, own]
-
-    def put_out(part, value):
-        out_ref[part] = value.astype(jnp.bfloat16)
+            join(last)
+
+        put_out(slot_end, lead_part)
+        put_out(slot_end, next_part)
+
+    def put_last(part, value):
+        state[levels, part, mine] = value.astype(jnp.bfloat16)
+        put_out(levels, part)
 
     @pl.when(group >= half)
     def _():
-        own_star(
-            parts(land.at[last]), parts(state.at[last]), put_out,
-            functools.partial(relay_first, last),
-            functools.partial(relay_second, last),
-            functools.partial(relay_end, last),
-            lambda step: (join_second, join_end)[step](last),
-        )
+        star(parts(land.at[last]), parts(state.at[last]), put_last, last)
+
+    for part in (3 - lead_part, 3 - next_part):
+        swap_copy(0, part).wait_recv()
 
     for layer in range(lay):
         for_offsets(lambda offset: mode_copy(offset, layer).wait_send())
@@ -372,7 +408,7 @@
         def _(level=level):
             far_left(level)
 
-        @pl.when(group >= reach)
+        @pl.when(jnp.logical_and(group >= reach, role == 0))
         def _(level=level):
             for part in (2, 3):
                 for piece in range(HALVES):
@@ -380,12 +416,17 @@
                     relay_copy(level, part, piece, 1, blk, sib).wait_send()
                     relay_copy(level, part, piece, 2, cross, sib).wait_send()
 
-        @pl.when(2 * group >= reach if level else group >= 0)
+        formed = 2 * group >= reach if level else group >= 0
+
+        @pl.when(jnp.logical_and(formed, role == 1))
         def _(level=level):
             for part in range(2):
                 join_copy(level, part, 0, blk, cross).wait_send()
                 join_copy(level, part, 1, blk, sib).wait_send()
                 join_copy(level, part, 2, cross, sib).wait_send()
+
+    for part in (lead_part, next_part):
+        swap_copy(0, part).wait_send()
 
 
 def on_device(n, nb, mode_matrix, decay_rate, facet_refl):
@@ -418,17 +459,18 @@
             pltpu.VMEM(square, jnp.bfloat16),
             pltpu.VMEM((2,) + square, jnp.bfloat16),
             pltpu.VMEM((lay, 3) + square, jnp.bfloat16),
-            pltpu.VMEM((levels, 4) + square, jnp.bfloat16),
+            pltpu.VMEM((levels + 1, 4) + square, jnp.bfloat16),
             pltpu.VMEM((levels, 4) + square, jnp.bfloat16),
         ]
-        + [pltpu.VMEM(square, jnp.bfloat16)] * 2
-        + [pltpu.VMEM((harm // nb, harm), jnp.bfloat16)] * 3
+        + [pltpu.VMEM(square, jnp.bfloat16)]
+        + [pltpu.VMEM((harm // 2, harm), jnp.bfloat16)] * 2
         + [dma((n, lay))] * 2
         + [dma((n,))] * 2
         + [dma((lay, n, 3))] * 2
         + [dma((levels, 4, HALVES))] * 2
         + [dma((levels, 4, HALVES, 3))] * 2
-        + [dma((levels, 2, 3))] * 2,
+        + [dma((levels, 2, 3))] * 2
+        + [dma((4,))] * 2,
         compiler_params=pltpu.CompilerParams(
             collective_id=0, has_side_effects=True, vmem_limit_bytes=56 * 1024 * 1024
         ),

time: 82 us -> 84.5 us (1.030)
  Pallas kernels: 77.5 us -> 80.9 us
    pallas_call x1, Pallas kernels: 77.5 us -> 80.9 us  [on_device(): pl.pallas_call(functools.partial(stack_kernel, n, nb, levels), out_shape=...]
where the time goes in v6:
time: 84.5 us; the launch traced here: 84.2 us
  Pallas kernels  80.9 us (96%)
  local copies, waits for them, and re-layouts  2.69 us (3%)
    pallas_call x1, Pallas kernels, on_device(): pl.pallas_call(functools.partial(stack_kernel, n, nb, levels), out_shape=...  80.9 us
    unnamed x5, local copies, waits for them, and re-layouts  2.56 us

profile of v6, /device:TPU:28, one launch (start us, length us, event | category | flops | bytes accessed | tf_op | source)
XLA Modules:
  0.0 84.2 jit_solution(18442365477231570517)
XLA Ops:
  0.0 0.0 copy-start.1
  0.0 0.0 copy-start
  0.0 0.7 copy-done.1
  0.7 0.0 copy-done
  0.8 0.1 tile.10
  0.9 0.6 broadcast_select_fusion.aux_ref
  1.5 80.9 %shard_map.37 = bf16[4,128,512]{2,1,0:T(8,128)(2,1)} custom-call(bf16[16,64,128]{2,1,0:T(8,128)(2,1)} %mode_ref.1, f32[8,8,128]{2,1,0:T(8,128)} %broadcast_select_fusion.aux_ref), custom_call_target="tpu_custom_call" | custom-call | flops 16106127360 | bytes 1048576 | tf_op jit(solution)/shard_map/pallas_call | solution.py:451
  82.4 1.9 %copy.5 = bf16[1,4,128,512]{3,2,1,0:T(8,128)(2,1)} copy(bf16[1,4,128,512]{3,2,1,0:T(8,128)(2,1)} %bitcast.4) | data formatting | bytes 1048576
  (5 shorter events, 0.1 us)
Async XLA Ops:
  0.0 0.7 copy-start.1
  0.0 0.7 copy-start

commit v7 on v4

--- a/solution.py
+++ b/solution.py
@@ -245,7 +245,7 @@
         source = start if repeat == 0 else total
         total[...] = (start[...] + dot(source[...], coupling[...])).astype(jnp.bfloat16)
 
-    def own_star(upper, lower, put, first, second, end, join):
+    def own_star(upper, lower, put, first, second, end, join, ahead):
         a11, a12, a21, a22 = upper
         b11, b12, b21, b22 = lower
         a11, a12, b21, b22 = [ref.at[own] for ref in (a11, a12, b21, b22)]
@@ -255,22 +255,25 @@
         join(1)
         end(3)
         up[...] = dot(a22[...], b11[...]).astype(jnp.bfloat16)
-        for repeat in range(REFL):
+        chain(right, b21, up, 0)
+        first(2)
+        for repeat in range(1, REFL):
             chain(right, b21, up, repeat)
         mid[...] = dot(right[...], a22[...]).astype(jnp.bfloat16)
         put(3, b22[...] + dot(mid[...], b12[...]))
+        second(2)
         down[...] = dot(b11[...], a22[...]).astype(jnp.bfloat16)
+        end(2)
+        put(2, dot(right[...], a21[...]))
         first(1)
-        first(2)
+        ahead(0)
         for repeat in range(REFL):
             chain(left, a12, down, repeat)
         put(1, dot(left[...], b12[...]))
         mid[...] = dot(left[...], b11[...]).astype(jnp.bfloat16)
-        second(2)
-        end(2)
-        put(2, dot(right[...], a21[...]))
         first(0)
         put(0, a11[...] + dot(mid[...], a21[...]))
+        ahead(1)
 
     def parts(ref):
         return [ref.at[part] for part in range(4)]
@@ -294,11 +297,18 @@
         return put
 
     own_star(
-        layer_parts(0), layer_parts(1), put_state(0, 1), nothing, nothing, nothing, nothing
+        layer_parts(0), layer_parts(1), put_state(0, 1), nothing, nothing, nothing, nothing,
+        nothing,
     )
 
     slot_end = sum(jnp.where(group >= (1 << k), 1, 0) for k in range(last))
     half = 1 << last
+    middle = jnp.logical_and(group >= half, 2 * group < 3 * half)
+    not_middle = jnp.logical_not(middle)
+
+    def relay_ahead(step):
+        for part in (3, 2):
+            (relay_first, relay_second)[step](last, part)
 
     def one_level(level, distance):
         @pl.when(group >= distance)
@@ -309,6 +319,9 @@
                 functools.partial(relay_second, level),
                 functools.partial(relay_end, level),
                 lambda step: (join_second, join_end)[step](level),
+                lambda step: pl.when(jnp.logical_and(level == last - 1, middle))(
+                    lambda: relay_ahead(step)
+                ),
             )
 
         @pl.when(group < distance)
@@ -322,14 +335,14 @@
 
             @pl.when(level == last - 2)
             def _():
-                for part in (3, 1):
+                for part in (3, 2):
                     send_far(last, half, slot_end, part)
 
-            for part in (3, 1):
+            for part in (3, 2):
                 @pl.when(jnp.logical_or(level < last - 1, 4 * group >= half))
                 def _(part=part):
                     send_far(level + 1, 2 * distance, slot_end, part)
-            for part in (2, 0):
+            for part in (1, 0):
                 send_far(level + 1, 2 * distance, slot_end, part)
 
         return 2 * distance
@@ -343,19 +356,26 @@
             join_second(last)
             join_end(last)
 
-        out_ref[...] = state[slot_end, :, own]
+        out_ref[...] = -state[slot_end, :, own]
 
     def put_out(part, value):
-        out_ref[part] = value.astype(jnp.bfloat16)
+        out_ref[part] = -value.astype(jnp.bfloat16)
+
+    def last_first(part):
+        if part >= 2:
+            pl.when(not_middle)(lambda: relay_first(last, part))
+        else:
+            relay_first(last, part)
 
     @pl.when(group >= half)
     def _():
         own_star(
             parts(land.at[last]), parts(state.at[last]), put_out,
-            functools.partial(relay_first, last),
-            functools.partial(relay_second, last),
+            last_first,
+            lambda part: pl.when(not_middle)(lambda: relay_second(last, part)),
             functools.partial(relay_end, last),
             lambda step: (join_second, join_end)[step](last),
+            nothing,
         )
 
     for layer in range(lay):
@@ -436,7 +456,7 @@
             flops=2 * harm**3 * 60, bytes_accessed=2**20, transcendentals=0
         ),
     )(mode_matrix, aux)
-    return result[None]
+    return -result[None]
 
 
 def solution(mesh):

time: 82 us -> 86.3 us (1.052)
  Pallas kernels: 77.5 us -> 81.8 us
  local copies, waits for them, and re-layouts: 2.69 us -> 0.82 us
  other arithmetic: 0.66 us -> 2.53 us
    pallas_call x1, Pallas kernels: 77.5 us -> 81.8 us  [on_device(): pl.pallas_call(functools.partial(stack_kernel, n, nb, levels), out_shape=...]
    neg x0 -> x1, other arithmetic: none -> 1.87 us  [on_device(): return -result[None]]
    unnamed x5 -> x4, local copies, waits for them, and re-layouts: 2.56 us -> 0.69 us
where the time goes in v7:
time: 86.3 us; the launch traced here: 85.1 us
  Pallas kernels  81.8 us (95%)
  other arithmetic  2.53 us (3%)
    pallas_call x1, Pallas kernels, on_device(): pl.pallas_call(functools.partial(stack_kernel, n, nb, levels), out_shape=...  81.8 us
    neg x1, other arithmetic, on_device(): return -result[None]  1.87 us

profile of v7, /device:TPU:28, one launch (start us, length us, event | category | flops | bytes accessed | tf_op | source)
XLA Modules:
  0.0 85.1 jit_solution(7347976864988914310)
XLA Ops:
  0.0 0.0 copy-start.1
  0.0 0.0 copy-start
  0.0 0.7 copy-done.1
  0.7 0.0 copy-done
  0.8 0.1 tile.10
  0.9 0.6 broadcast_select_fusion.aux_ref
  1.5 81.8 %shard_map.37 = bf16[4,128,512]{2,1,0:T(8,128)(2,1)} custom-call(bf16[16,64,128]{2,1,0:T(8,128)(2,1)} %mode_ref.1, f32[8,8,128]{2,1,0:T(8,128)} %broadcast_select_fusion.aux_ref), custom_call_target="tpu_custom_call" | custom-call | flops 16106127360 | bytes 1048576 | tf_op jit(solution)/shard_map/pallas_call | solution.py:430
  83.3 1.9 %negate_bitcast_fusion = bf16[1,4,128,512]{3,2,1,0:T(8,128)(2,1)} fusion(bf16[4,128,512]{2,1,0:T(8,128)(2,1)} %shard_map.37), kind=kLoop, calls=%fused_computation | loop fusion | flops 262144 | bytes 1048576 | tf_op jit(solution)/shard_map/neg | solution.py:459
  (5 shorter events, 0.1 us)
Async XLA Ops:
  0.0 0.7 copy-start.1
  0.0 0.7 copy-start

commit v8 on v6

--- a/solution.py
+++ b/solution.py
@@ -202,33 +202,21 @@
         for half in range(HALVES):
             far_copy(level, 1, 0, part, half).wait_recv()
 
-    def join_copy(slot, part, index, device, other):
-        where = state.at[slot, part, wing_of(device)]
-        return pltpu.make_async_remote_copy(
-            src_ref=where,
-            dst_ref=where,
-            send_sem=join_send.at[slot, part, index],
-            recv_sem=join_recv.at[slot, part, index],
-            device_id=(group, other),
-            device_id_type=MESH,
-        )
-
-    def join_first(slot, part):
-        join_copy(slot, part, 0, blk, cross).start()
-        join_copy(slot, part, 1, blk, sib).start()
-
-    def join_second(slot):
-        for part in (1, 0):
-            join_copy(slot, part, 0, cross, cross).wait_recv()
-            join_copy(slot, part, 2, cross, sib).start()
+    def join_copy(slot, part):
+        return pltpu.make_async_remote_copy(
+            src_ref=state.at[slot, part],
+            dst_ref=state.at[slot, part],
+            send_sem=join_send.at[slot, part],
+            recv_sem=join_recv.at[slot, part],
+            device_id=(group, sib),
+            device_id_type=MESH,
+        )
 
     def join_end(slot):
         for part in (1, 0):
-            join_copy(slot, part, 1, sib, sib).wait_recv()
-            join_copy(slot, part, 2, sib_cross, sib).wait_recv()
+            join_copy(slot, part).wait_recv()
 
     def join(slot):
-        pl.when(role == 1)(lambda: join_second(slot))
         pl.when(role == 0)(lambda: join_end(slot))
 
     def relay_copy(level, part, half, index, device, other):
@@ -248,6 +236,15 @@
             relay_copy(level, part, half, 0, blk, cross).start()
             relay_copy(level, part, half, 1, blk, sib).start()
 
+    def near_first(level, part):
+        for half in range(HALVES):
+            far_copy(level, 1, 0, part, half).wait_recv()
+            relay_copy(level, part, half, 0, blk, cross).start()
+
+    def near_end(level, part):
+        for half in range(HALVES):
+            relay_copy(level, part, half, 0, cross, cross).wait_recv()
+
     def relay_second(level, part):
         for half in range(HALVES):
             relay_copy(level, part, half, 0, cross, cross).wait_recv()
@@ -276,49 +273,63 @@
         source = start if repeat == 0 else total
         total[...] = (start[...] + dot(source[...], coupling[...])).astype(jnp.bfloat16)
 
-    def under_star(upper, lower, put, level):
+    def under_star(upper, lower, put, level, rows_now, final):
         a11, a12, a21, a22 = upper
         b11, b12, b21, b22 = lower
-        b21, b22 = b21.at[mine], b22.at[mine]
+        b21, b22 = b21.at[rows_now], b22.at[rows_now]
+        acc, part_mid = total.at[: b21.shape[0]], mid.at[: b21.shape[0]]
         if level is not None:
             relay_first(level, 3)
             join_end(level)
             relay_second(level, 3)
         up[...] = dot(a22[...], b11[...]).astype(jnp.bfloat16)
-        chain(total, b21, up, 0)
-        chain(total, b21, up, 1)
+        chain(acc, b21, up, 0)
+        chain(acc, b21, up, 1)
         if level is not None:
             relay_first(level, 2)
-        chain(total, b21, up, 2)
-        chain(total, b21, up, 3)
-        mid[...] = dot(total[...], a22[...]).astype(jnp.bfloat16)
-        put(3, b22[...] + dot(mid[...], b12[...]))
+        chain(acc, b21, up, 2)
+        chain(acc, b21, up, 3)
+        part_mid[...] = dot(acc[...], a22[...]).astype(jnp.bfloat16)
+        put(3, b22[...] + dot(part_mid[...], b12[...]))
         if level is not None:
             relay_second(level, 2)
-        put(2, dot(total[...], a21[...]))
-
-    def over_star(upper, lower, put, level):
+        put(2, dot(acc[...], a21[...]))
+
+    def over_star(upper, lower, put, level, rows_now, final):
         a11, a12, a21, a22 = upper
         b11, b12, b21, b22 = lower
-        a11, a12 = a11.at[mine], a12.at[mine]
+        a11, a12 = a11.at[rows_now], a12.at[rows_now]
+        acc, part_mid = total.at[: a11.shape[0]], mid.at[: a11.shape[0]]
         if level is not None:
-            join_second(level)
             relay_end(level, 3)
         up[...] = dot(b11[...], a22[...]).astype(jnp.bfloat16)
         if level is not None:
-            far_end(level, 1)
-        for repeat in range(REFL):
-            chain(total, a12, up, repeat)
-        put(1, dot(total[...], b12[...]))
-        mid[...] = dot(total[...], b11[...]).astype(jnp.bfloat16)
+            if final:
+                far_end(level, 1)
+            else:
+                near_first(level, 1)
+                near_end(level, 1)
+        chain(acc, a12, up, 0)
+        chain(acc, a12, up, 1)
+        if level is not None and not final:
+            near_first(level, 0)
+        chain(acc, a12, up, 2)
+        chain(acc, a12, up, 3)
+        put(1, dot(acc[...], b12[...]))
+        part_mid[...] = dot(acc[...], b11[...]).astype(jnp.bfloat16)
         if level is not None:
-            far_end(level, 0)
+            if final:
+                far_end(level, 0)
+            else:
+                near_end(level, 0)
             relay_end(level, 2)
-        put(0, a11[...] + dot(mid[...], a21[...]))
-
-    def star(upper, lower, put, level):
-        pl.when(role == 0)(lambda: under_star(upper, lower, put, level))
-        pl.when(role == 1)(lambda: over_star(upper, lower, put, level))
+        put(0, a11[...] + dot(part_mid[...], a21[...]))
+
+    def star(upper, lower, put, level, rows_now=slice(None), final=False):
+        for own_role, form in enumerate((under_star, over_star)):
+            pl.when(role == own_role)(
+                functools.partial(form, upper, lower, put, level, rows_now, final)
+            )
 
     def parts(ref):
         return [ref.at[part] for part in range(4)]
@@ -332,10 +343,10 @@
 
     def put_state(level, distance):
         def put(part, value):
-            state[level, part, mine] = value.astype(jnp.bfloat16)
+            state[level, part] = value.astype(jnp.bfloat16)
             send_far(level, distance, level, part)
             if part < 2:
-                join_first(level, part)
+                join_copy(level, part).start()
 
         return put
 
@@ -389,7 +400,7 @@
 
     @pl.when(group >= half)
     def _():
-        star(parts(land.at[last]), parts(state.at[last]), put_last, last)
+        star(parts(land.at[last]), parts(state.at[last]), put_last, last, mine, True)
 
     for part in (3 - lead_part, 3 - next_part):
         swap_copy(0, part).wait_recv()
@@ -416,14 +427,19 @@
                     relay_copy(level, part, piece, 1, blk, sib).wait_send()
                     relay_copy(level, part, piece, 2, cross, sib).wait_send()
 
+        if level < last:
+            @pl.when(jnp.logical_and(group >= reach, role == 1))
+            def _(level=level):
+                for part in range(2):
+                    for piece in range(HALVES):
+                        relay_copy(level, part, piece, 0, blk, cross).wait_send()
+
         formed = 2 * group >= reach if level else group >= 0
 
         @pl.when(jnp.logical_and(formed, role == 1))
         def _(level=level):
             for part in range(2):
-                join_copy(level, part, 0, blk, cross).wait_send()
-                join_copy(level, part, 1, blk, sib).wait_send()
-                join_copy(level, part, 2, cross, sib).wait_send()
+                join_copy(level, part).wait_send()
 
     for part in (lead_part, next_part):
         swap_copy(0, part).wait_send()
@@ -462,14 +478,13 @@
             pltpu.VMEM((levels + 1, 4) + square, jnp.bfloat16),
             pltpu.VMEM((levels, 4) + square, jnp.bfloat16),
         ]
-        + [pltpu.VMEM(square, jnp.bfloat16)]
-        + [pltpu.VMEM((harm // 2, harm), jnp.bfloat16)] * 2
+        + [pltpu.VMEM(square, jnp.bfloat16)] * 3
         + [dma((n, lay))] * 2
         + [dma((n,))] * 2
         + [dma((lay, n, 3))] * 2
         + [dma((levels, 4, HALVES))] * 2
         + [dma((levels, 4, HALVES, 3))] * 2
-        + [dma((levels, 2, 3))] * 2
+        + [dma((levels, 2))] * 2
         + [dma((4,))] * 2,
         compiler_params=pltpu.CompilerParams(
             collective_id=0, has_side_effects=True, vmem_limit_bytes=56 * 1024 * 1024

time: 84.5 us -> 88.8 us (1.051)
  Pallas kernels: 80.9 us -> 85.2 us
    pallas_call x1, Pallas kernels: 80.9 us -> 85.2 us  [on_device(): pl.pallas_call(functools.partial(stack_kernel, n, nb, levels), out_shape=...]
where the time goes in v8:
time: 88.8 us; the launch traced here: 88.6 us
  Pallas kernels  85.2 us (96%)
  local copies, waits for them, and re-layouts  2.69 us (3%)
    pallas_call x1, Pallas kernels, on_device(): pl.pallas_call(functools.partial(stack_kernel, n, nb, levels), out_shape=...  85.2 us
    unnamed x5, local copies, waits for them, and re-layouts  2.56 us

profile of v8, /device:TPU:28, one launch (start us, length us, event | category | flops | bytes accessed | tf_op | source)
XLA Modules:
  0.0 88.6 jit_solution(833077312963381352)
XLA Ops:
  0.0 0.0 copy-start.1
  0.0 0.0 copy-start
  0.0 0.7 copy-done.1
  0.7 0.0 copy-done
  0.8 0.1 tile.10
  0.9 0.6 broadcast_select_fusion.aux_ref
  1.5 85.2 %shard_map.37 = bf16[4,128,512]{2,1,0:T(8,128)(2,1)} custom-call(bf16[16,64,128]{2,1,0:T(8,128)(2,1)} %mode_ref.1, f32[8,8,128]{2,1,0:T(8,128)} %broadcast_select_fusion.aux_ref), custom_call_target="tpu_custom_call" | custom-call | flops 16106127360 | bytes 1048576 | tf_op jit(solution)/shard_map/pallas_call | solution.py:467
  86.8 1.9 %copy.5 = bf16[1,4,128,512]{3,2,1,0:T(8,128)(2,1)} copy(bf16[1,4,128,512]{3,2,1,0:T(8,128)(2,1)} %bitcast.4) | data formatting | bytes 1048576
  (5 shorter events, 0.1 us)
Async XLA Ops:
  0.0 0.7 copy-start.1
  0.0 0.7 copy-start

commit v9 on v4

--- a/solution.py
+++ b/solution.py
@@ -9,7 +9,7 @@
 
 REFL = 4
 LANES = 128
-HALVES = 2
+HALVES = 1
 MESH = pl.DeviceIdType.MESH
 
 

time: 82 us -> 82.6 us (level)
  Pallas kernels: 77.5 us -> 78.4 us
    pallas_call x1, Pallas kernels: 77.5 us -> 78.4 us  [on_device(): pl.pallas_call(functools.partial(stack_kernel, n, nb, levels), out_shape=...]
where the time goes in v9:
time: 82.6 us; the launch traced here: 81.8 us
  Pallas kernels  78.4 us (95%)
  local copies, waits for them, and re-layouts  2.69 us (3%)
    pallas_call x1, Pallas kernels, on_device(): pl.pallas_call(functools.partial(stack_kernel, n, nb, levels), out_shape=...  78.4 us
    unnamed x5, local copies, waits for them, and re-layouts  2.56 us

profile of v9, /device:TPU:28, one launch (start us, length us, event | category | flops | bytes accessed | tf_op | source)
XLA Modules:
  0.0 81.8 jit_solution(13840105060261133339)
XLA Ops:
  0.0 0.0 copy-start.1
  0.0 0.0 copy-start
  0.0 0.7 copy-done.1
  0.7 0.0 copy-done
  0.8 0.1 tile.10
  0.9 0.6 broadcast_select_fusion.aux_ref
  1.5 78.4 %shard_map.37 = bf16[4,128,512]{2,1,0:T(8,128)(2,1)} custom-call(bf16[16,64,128]{2,1,0:T(8,128)(2,1)} %mode_ref.1, f32[8,8,128]{2,1,0:T(8,128)} %broadcast_select_fusion.aux_ref), custom_call_target="tpu_custom_call" | custom-call | flops 16106127360 | bytes 1048576 | tf_op jit(solution)/shard_map/pallas_call | solution.py:410
  79.9 1.9 %copy.5 = bf16[1,4,128,512]{3,2,1,0:T(8,128)(2,1)} copy(bf16[1,4,128,512]{3,2,1,0:T(8,128)(2,1)} %bitcast.4) | data formatting | bytes 1048576
  (5 shorter events, 0.1 us)
Async XLA Ops:
  0.0 0.7 copy-start.1
  0.0 0.7 copy-start
